TPU v7x, 256 devices: a whole 4x4x8 slice. The times are simulated.
256 devices in a mesh: expert: 32 (over y_hi, z, core), dp: 8 (over x, y_lo).
Axes of the slice: x: 4, y: 4 (y_hi: 2, y_lo: 2; y = y_hi * 2 + y_lo), z: 8, core: 2. Of those that a mesh axis runs over, the one named last changes fastest.
Arguments:
- tokens: bfloat16 [32768, 2048], P(('expert', 'dp')), may hold values from -6 to 6
- out_grad: bfloat16 [32768, 2048], P(('expert', 'dp')), may hold values from -0.0059814453 to 0.0059814453
- saved_pre: bfloat16 [32768, 8, 1024], P(('expert', 'dp')), may hold values from -6 to 6
- router_weight: float32 [2048, 64], replicated, may hold values from -0.125 to 0.125
- slot_expert: int32 [256], replicated, may hold values from 0 to 63, as said below
- slot_of: int32 [32768, 8], P(('expert', 'dp')), may hold values from 0 to 255, as said below
- slot_weight: bfloat16 [256, 2048, 1536], P(('expert', 'dp')), as said below
Outputs:
- token_grad: bfloat16 [32768, 2048], P(('expert', 'dp'))
- expert_grads: bfloat16 [2048, 64, 1536], P('dp', 'expert')
- router_grad: float32 [2048, 64], replicated
Inputs may be any that keep to these rules, and one draw needn't show every extreme that they name: `slot_expert`: slots 8 * c to 8 * c + 7 hold experts 2 c and 2 c + 1, each on at least one slot; one of the two holds the lower slots of the group, the other the higher ones. `slot_of`: the 8 slots of a token lie in distinct groups of 8 slots. The 128 tokens of one device name each group exactly 32 times and no slot more than 5 times; in every group one slot is named exactly 5 times by every device's tokens. `slot_weight`: slots that hold the same expert hold the same weights.
All inputs are finite; a program needn't handle non-finite values.
Results may differ from a plain program's by a relative error of at most 0.01.
Values may be sent and summed in bfloat16 or wider, within the bound.
A program may use at most 128 MiB of HBM per device.

v0:
```python
import jax
import jax.numpy as jnp
from jax import lax
from jax.sharding import PartitionSpec as P

zloss_coef = 0.001
balance_coef = 0.01


def expert_rows(upstream, saved_rows, route_weight, matrix):
    hidden_width = saved_rows.shape[1] // 2
    gate_pre = saved_rows[:, :hidden_width].astype(jnp.float32)
    upward = saved_rows[:, hidden_width:].astype(jnp.float32)
    sigmoid_gate = jax.nn.sigmoid(gate_pre)
    active = gate_pre * sigmoid_gate
    hidden = active * upward
    weight_col = route_weight.astype(jnp.float32)[:, None]
    back_grad = jnp.dot(upstream, matrix[:, 2 * hidden_width :], preferred_element_type=jnp.float32)
    prob_grad = jnp.sum(back_grad * hidden, axis=1).astype(jnp.bfloat16)
    scaled = (weight_col * hidden).astype(jnp.bfloat16)
    hidden_grad = weight_col * back_grad
    gate_grad = hidden_grad * upward * sigmoid_gate * (1.0 + gate_pre * (1.0 - sigmoid_gate))
    pre_grad = jnp.concatenate([gate_grad, hidden_grad * active], axis=1).astype(jnp.bfloat16)
    part_grad = lax.dot_general(
        pre_grad,
        matrix[:, : 2 * hidden_width],
        (((1,), (1,)), ((), ())),
        preferred_element_type=jnp.float32,
    ).astype(jnp.bfloat16)
    return (part_grad, prob_grad, pre_grad, scaled)


def slot_gradient(inputs, upstream, pre_grad, scaled):
    first = lax.dot_general(
        inputs, pre_grad, (((0,), (0,)), ((), ())), preferred_element_type=jnp.float32
    )
    second = lax.dot_general(
        upstream, scaled, (((0,), (0,)), ((), ())), preferred_element_type=jnp.float32
    )
    return jnp.concatenate([first, second], axis=1).astype(jnp.bfloat16)


def local(tokens, out_grad, saved_pre, router_weight, slot_expert, slot_of, slot_weight):
    group_count = lax.axis_size("expert")
    data_count = lax.axis_size("dp")
    tok_rows = tokens.shape[0]
    model_width = tokens.shape[1]
    per_token = slot_of.shape[1]
    hidden_width = saved_pre.shape[2] // 2
    expert_count = router_weight.shape[1]
    slot_count = slot_expert.shape[0]
    per_group = expert_count // group_count
    column_quota = tok_rows * per_token // group_count
    capacity = column_quota // data_count + max(1, column_quota // (4 * data_count))
    assign_count = tok_rows * per_token
    slot_flat = slot_of.reshape(-1)
    slot_match = slot_flat[:, None] == jnp.arange(slot_count, dtype=jnp.int32)[None, :]
    expert_flat = jnp.sum(jnp.where(slot_match, slot_expert[None, :], 0), axis=1)
    expert_ids = expert_flat.reshape(tok_rows, per_token)
    arrival = jnp.sum(jnp.cumsum(slot_match.astype(jnp.int32), axis=0) * slot_match, axis=1) - 1
    target = slot_flat * capacity + arrival
    source = (
        jnp.full((slot_count * capacity,), -1, jnp.int32)
        .at[target]
        .set(jnp.arange(assign_count, dtype=jnp.int32))
    )
    filled = source >= 0
    chosen_row = jnp.maximum(source, 0)
    owner_row = chosen_row // per_token
    wide_tokens = tokens.astype(jnp.float32)
    logits = jnp.dot(wide_tokens, router_weight, precision=lax.Precision.HIGHEST)
    log_total = jax.nn.logsumexp(logits, axis=1)
    router_probs = jnp.exp(logits - log_total[:, None])
    chosen = expert_ids[:, :, None] == jnp.arange(expert_count, dtype=jnp.int32)[None, None, :]
    chosen_prob = jnp.sum(jnp.where(chosen, router_probs[:, None, :], 0.0), axis=2).astype(
        jnp.bfloat16
    )
    counts = jnp.sum(chosen.astype(jnp.int32), axis=(0, 1))
    zero_half = jnp.zeros((), jnp.bfloat16)
    lead_shape = (group_count, data_count)
    send_tokens = jnp.where(filled[:, None], tokens[owner_row], zero_half).reshape(
        lead_shape + (capacity * model_width,)
    )
    send_grads = jnp.where(filled[:, None], out_grad[owner_row], zero_half).reshape(
        lead_shape + (capacity * model_width,)
    )
    saved_flat = saved_pre.reshape(assign_count, 2 * hidden_width)
    send_saved = jnp.where(filled[:, None], saved_flat[chosen_row], zero_half).reshape(
        lead_shape + (capacity * 2 * hidden_width,)
    )
    send_weight = jnp.where(filled, chosen_prob.reshape(-1)[chosen_row], zero_half).reshape(
        lead_shape + (capacity,)
    )
    arrived = (
        lax.all_to_all(
            lax.all_to_all(send_tokens, "expert", split_axis=0, concat_axis=0, tiled=True),
            "dp",
            split_axis=1,
            concat_axis=1,
            tiled=True,
        ),
        lax.all_to_all(
            lax.all_to_all(send_grads, "expert", split_axis=0, concat_axis=0, tiled=True),
            "dp",
            split_axis=1,
            concat_axis=1,
            tiled=True,
        ),
        lax.all_to_all(
            lax.all_to_all(send_saved, "expert", split_axis=0, concat_axis=0, tiled=True),
            "dp",
            split_axis=1,
            concat_axis=1,
            tiled=True,
        ),
        lax.all_to_all(
            lax.all_to_all(send_weight, "expert", split_axis=0, concat_axis=0, tiled=True),
            "dp",
            split_axis=1,
            concat_axis=1,
            tiled=True,
        ),
    )
    slot_rows = slot_count * capacity
    inputs = arrived[0].reshape(slot_rows, model_width)
    upstream = arrived[1].reshape(slot_rows, model_width)
    saved_rows = arrived[2].reshape(slot_rows, 2 * hidden_width)
    route_weight = arrived[3].reshape(slot_rows)
    matrix = slot_weight[0]
    part_grad, prob_grad, pre_grad, scaled = expert_rows(upstream, saved_rows, route_weight, matrix)
    part_send = part_grad.reshape(lead_shape + (capacity * model_width,))
    prob_send = prob_grad.reshape(lead_shape + (capacity,))
    returned = (
        lax.all_to_all(
            lax.all_to_all(part_send, "expert", split_axis=0, concat_axis=0, tiled=True),
            "dp",
            split_axis=1,
            concat_axis=1,
            tiled=True,
        ),
        lax.all_to_all(
            lax.all_to_all(prob_send, "expert", split_axis=0, concat_axis=0, tiled=True),
            "dp",
            split_axis=1,
            concat_axis=1,
            tiled=True,
        ),
    )
    part_back = (
        returned[0]
        .reshape(slot_rows, model_width)[target]
        .reshape(tok_rows, per_token, model_width)
    )
    expert_part = jnp.sum(part_back.astype(jnp.float32), axis=1)
    prob_back = (
        returned[1].reshape(slot_rows)[target].astype(jnp.float32).reshape(tok_rows, per_token)
    )
    group_index = lax.axis_index("expert")
    data_index = lax.axis_index("dp")
    group_base = group_index * per_group
    row_share = model_width // data_count
    own_lane = slot_expert[group_index * data_count + data_index] - group_base
    lane_mask = (jnp.arange(per_group, dtype=jnp.int32) == own_lane)[None, :, None]
    piece = slot_gradient(inputs, upstream, pre_grad, scaled)
    piece = lax.optimization_barrier(piece).astype(jnp.float32)
    spread = jnp.where(lane_mask, piece[:, None, :], 0.0)
    summed = lax.psum_scatter(
        spread.reshape(row_share * lax.axis_size("dp"), per_group * 3 * hidden_width).astype(
            jnp.bfloat16
        ),
        "dp",
        scatter_dimension=0,
        tiled=True,
    ).astype(jnp.float32)
    expert_grads = summed.reshape(row_share, per_group, 3 * hidden_width).astype(jnp.bfloat16)
    probs_grad = jnp.sum(jnp.where(chosen, prob_back[:, :, None], 0.0), axis=1)
    probs_grad = probs_grad + balance_coef * expert_count * counts.astype(jnp.float32) / (
        tok_rows * per_token
    )
    inner = jnp.sum(router_probs * probs_grad, axis=1, keepdims=True)
    logits_grad = (
        router_probs * (probs_grad - inner) + 2.0 * zloss_coef * log_total[:, None] * router_probs
    )
    local_router = jnp.dot(wide_tokens.T, logits_grad, precision=lax.Precision.HIGHEST)
    router_grad = lax.psum(local_router, ("expert", "dp"))
    router_part = jnp.dot(logits_grad, router_weight.T, precision=lax.Precision.HIGHEST)
    token_grad = (expert_part + router_part).astype(jnp.bfloat16)
    return (token_grad, expert_grads, router_grad)


def solution(mesh):
    placed = (
        P(("expert", "dp"), None),
        P(("expert", "dp"), None),
        P(("expert", "dp"), None, None),
        P(),
        P(),
        P(("expert", "dp"), None),
        P(("expert", "dp"), None, None),
    )
    return jax.shard_map(
        local,
        mesh=mesh,
        in_specs=placed,
        out_specs=(P(("expert", "dp"), None), P("dp", "expert", None), P()),
        check_vma=False,
    )
```

profile of v0, /device:TPU:2, one launch (start us, length us, event | category | flops | bytes accessed | tf_op | source)
XLA Modules:
  0.0 1283.3 jit_solution(13823455707029847212)
XLA Ops:
  11.4 4.3 scatter_custom_fusion
  16.3 5.1 gather_fusion.2
  21.4 5.5 gather.28
  27.3 3.5 broadcast_select_fusion.2
  30.7 11.7 all-to-all-start.4
  42.5 6.1 gather_fusion.5
  48.6 9.4 gather.32
  58.0 6.1 gather_fusion.1
  64.1 9.4 gather.26
  73.5 2.2 broadcast_in_dim.136
  75.7 9.6 broadcast_select_fusion
  85.3 20.3 %all-to-all-done.4 = bf16[32,8,5120]{2,1,0:T(8,128)(2,1)} async-done(((bf16[32,8,5120]{2,1,0:T(8,128)(2,1)}), bf16[32,8,5120]{2,1,0:T(8,128)(2,1)}, u32[]{:S(2)}, u32[]{:S(2)}) %all-to-all-start.4) | async-done | bytes 2621472 | tf_op jit(solution)/shard_map/all_to_all | solution.py:110
  105.6 5.6 all-to-all-start.2
  111.2 4.6 copy.129
  115.9 114.9 %all-to-all-done.2 = bf16[32,8,10240]{2,1,0:T(8,128)(2,1)} async-done(((bf16[32,8,10240]{2,1,0:T(8,128)(2,1)}), bf16[32,8,10240]{2,1,0:T(8,128)(2,1)}, u32[]{:S(2)}, u32[]{:S(2)}) %all-to-all-start.2) | async-done | bytes 5242912 | tf_op jit(solution)/shard_map/all_to_all | solution.py:103
  230.8 4.9 all-to-all-start.5
  235.7 7.6 copy.126
  243.4 27.2 %all-to-all-done.5 = bf16[32,8,5120]{2,0,1:T(8,128)(2,1)} async-done(((bf16[32,8,5120]{2,0,1:T(8,128)(2,1)}), bf16[32,8,5120]{2,0,1:T(8,128)(2,1)}, u32[]{:S(2)}, u32[]{:S(2)}) %all-to-all-start.5) | async-done | bytes 2621472 | tf_op jit(solution)/shard_map/all_to_all | solution.py:109
  270.6 7.7 all-to-all-start.3
  278.3 4.6 copy.130
  282.9 5.5 reshape.158
  288.4 1.9 fusion.21
  290.3 1.4 copy.142
  292.3 55.2 %all-to-all-done.3 = bf16[32,8,10240]{2,0,1:T(8,128)(2,1)} async-done(((bf16[32,8,10240]{2,0,1:T(8,128)(2,1)}), bf16[32,8,10240]{2,0,1:T(8,128)(2,1)}, u32[]{:S(2)}, u32[]{:S(2)}) %all-to-all-start.3) | async-done | bytes 5242912 | tf_op jit(solution)/shard_map/all_to_all | solution.py:102
  347.6 7.6 copy.127
  355.2 9.5 reshape.156
  364.7 8.2 multiply_reduce_fusion
  373.1 18.5 %all_to_all.60 = bf16[32,8,5]{2,1,0:T(8,128)(2,1)S(1)} all-to-all(bf16[32,8,5]{2,1,0:T(8,128)(2,1)S(1)} %convert_element_type.96), channel_id=1, replica_groups=mesh['expert'=32,'dp'=8] {'expert'}, dimensions={0} | all-to-all | bytes 5120 | tf_op jit(solution)/shard_map/all_to_all | solution.py:142
  391.8 10.7 all_to_all.61
  402.5 5.1 all-to-all-start.10
  407.7 1.7 fusion.22
  409.9 6.8 gather_fusion.4
  417.2 8.0 gather_fusion
  426.1 101.1 %all-to-all-done.10 = bf16[32,8,10240]{2,1,0:T(8,128)(2,1)} async-done(((bf16[32,8,10240]{2,1,0:T(8,128)(2,1)}), bf16[32,8,10240]{2,1,0:T(8,128)(2,1)}, u32[]{:S(2)}, u32[]{:S(2)}) %all-to-all-start.10) | async-done | bytes 5242912 | tf_op jit(solution)/shard_map/all_to_all | solution.py:96
  527.1 7.0 all-to-all-start
  534.1 7.7 copy.138
  541.9 2.9 all-to-all-done
  544.7 6.0 all-to-all-start.11
  552.7 68.2 %all-to-all-done.11 = bf16[32,8,10240]{2,0,1:T(8,128)(2,1)} async-done(((bf16[32,8,10240]{2,0,1:T(8,128)(2,1)}), bf16[32,8,10240]{2,0,1:T(8,128)(2,1)}, u32[]{:S(2)}, u32[]{:S(2)}) %all-to-all-start.11) | async-done | bytes 5242912 | tf_op jit(solution)/shard_map/all_to_all | solution.py:95
  621.0 6.5 all-to-all-start.1
  627.6 7.7 copy.139
  635.3 9.7 reshape.162
  645.4 6.1 convolution_convert_fusion.2
  654.5 6.6 convolution_convert_fusion.1
  661.1 3.5 pad_maximum_fusion
  664.5 8.7 copy.140
  673.2 9.2 broadcast_in_dim.147
  682.4 8.8 copy.143
  691.2 7.0 select_convert_fusion
  699.9 9.8 convolution_convert_fusion
  709.6 9.5 reshape.159
  719.1 128.0 %all_to_all.62 = bf16[32,8,10240]{2,1,0:T(8,128)(2,1)S(1)} all-to-all(bf16[32,8,10240]{2,1,0:T(8,128)(2,1)} %reshape.159), channel_id=1, replica_groups=mesh['expert'=32,'dp'=8] {'expert'}, dimensions={0} | all-to-all | bytes 10485760 | tf_op jit(solution)/shard_map/all_to_all | solution.py:135
  847.1 5.2 copy.133
  852.3 5.1 all-to-all-start.7
  858.9 89.4 %all-to-all-done.7 = bf16[32,8,10240]{2,0,1:T(8,128)(2,1)} async-done(((bf16[32,8,10240]{2,0,1:T(8,128)(2,1)}), bf16[32,8,10240]{2,0,1:T(8,128)(2,1)}, u32[]{:S(2)}, u32[]{:S(2)}) %all-to-all-start.7) | async-done | bytes 5242912 | tf_op jit(solution)/shard_map/all_to_all | solution.py:134
  948.3 7.7 copy.134
  956.0 9.5 reshape.160
  965.6 12.0 gather_fusion.3
  977.6 5.2 convert_reduce_fusion
  982.9 1.9 fusion.8
  984.8 76.7 %reduce-scatter.2.cloned.1.call-done = bf16[256,3072]{1,0:T(8,128)(2,1)} async-done(((bf16[2048,3072]{1,0:T(8,128)(2,1)}), bf16[256,3072]{1,0:T(8,128)(2,1)}) %reduce-scatter.2.cloned.1.call-update) | async-done | bytes 1572880 | tf_op jit(solution)/shard_map/reduce_scatter | solution.py:167
  1061.5 5.0 convert_element_type.105
  1066.5 207.2 %all-reduce.2.cloned.1.call-done = f32[2048,64]{0,1:T(8,128)} async-done(((f32[2048,64]{0,1:T(8,128)}), f32[2048,64]{0,1:T(8,128)}) %all-reduce.2.cloned.1.call-update) | async-done | bytes 524304 | tf_op jit(solution)/shard_map/psum | solution.py:185
  1273.7 1.9 copy.146
  (86 shorter events, 15.0 us)
Async XLA Ops:
  8.0 8.3 copy-start
  10.1 0.7 copy-start.12
  30.7 11.7 copy-start.2
  30.7 74.9 %all-to-all-start.4 = ((bf16[32,8,5120]{2,1,0:T(8,128)(2,1)}), bf16[32,8,5120]{2,1,0:T(8,128)(2,1)}, u32[]{:S(2)}, u32[]{:S(2)}) async-start(bf16[32,8,5120]{2,1,0:T(8,128)(2,1)} %broadcast_select_fusion.2), calls=%async_computation.4 | async-start | bytes 5242880 | tf_op jit(solution)/shard_map/all_to_all | solution.py:110
  48.6 9.4 copy-start.3
  105.6 125.2 %all-to-all-start.2 = ((bf16[32,8,10240]{2,1,0:T(8,128)(2,1)}), bf16[32,8,10240]{2,1,0:T(8,128)(2,1)}, u32[]{:S(2)}, u32[]{:S(2)}) async-start(bf16[32,8,10240]{2,1,0:T(8,128)(2,1)} %get-tuple-element.12), calls=%async_computation.2 | async-start | bytes 10485760 | tf_op jit(solution)/shard_map/all_to_all | solution.py:103
  230.8 39.8 %all-to-all-start.5 = ((bf16[32,8,5120]{2,0,1:T(8,128)(2,1)}), bf16[32,8,5120]{2,0,1:T(8,128)(2,1)}, u32[]{:S(2)}, u32[]{:S(2)}) async-start(bf16[32,8,5120]{2,0,1:T(8,128)(2,1)} %copy.129), calls=%async_computation.5 | async-start | bytes 5242880 | tf_op jit(solution)/shard_map/all_to_all | solution.py:109
  270.6 77.0 %all-to-all-start.3 = ((bf16[32,8,10240]{2,0,1:T(8,128)(2,1)}), bf16[32,8,10240]{2,0,1:T(8,128)(2,1)}, u32[]{:S(2)}, u32[]{:S(2)}) async-start(bf16[32,8,10240]{2,0,1:T(8,128)(2,1)} %copy.126), calls=%async_computation.3 | async-start | bytes 10485760 | tf_op jit(solution)/shard_map/all_to_all | solution.py:102
  355.2 9.5 copy-start.5
  402.5 124.6 %all-to-all-start.10 = ((bf16[32,8,10240]{2,1,0:T(8,128)(2,1)}), bf16[32,8,10240]{2,1,0:T(8,128)(2,1)}, u32[]{:S(2)}, u32[]{:S(2)}) async-start(bf16[32,8,10240]{2,1,0:T(8,128)(2,1)} %get-tuple-element.11), calls=%async_computation.10 | async-start | bytes 10485760 | tf_op jit(solution)/shard_map/all_to_all | solution.py:96
  527.1 17.6 %all-to-all-start = ((bf16[32,8,5]{2,1,0:T(8,128)(2,1)}), bf16[32,8,5]{2,1,0:T(8,128)(2,1)S(1)}, u32[]{:S(2)}, u32[]{:S(2)}) async-start(bf16[32,8,5]{2,1,0:T(8,128)(2,1)} %reshape.155), calls=%async_computation | async-start | bytes 131072 | tf_op jit(solution)/shard_map/all_to_all | solution.py:117
  544.7 76.3 %all-to-all-start.11 = ((bf16[32,8,10240]{2,0,1:T(8,128)(2,1)}), bf16[32,8,10240]{2,0,1:T(8,128)(2,1)}, u32[]{:S(2)}, u32[]{:S(2)}) async-start(bf16[32,8,10240]{2,0,1:T(8,128)(2,1)} %copy.138), calls=%async_computation.11 | async-start | bytes 10485760 | tf_op jit(solution)/shard_map/all_to_all | solution.py:95
  621.0 24.1 %all-to-all-start.1 = ((bf16[32,8,5]{0,2,1:T(8,128)(2,1)}), bf16[32,8,5]{0,2,1:T(8,128)(2,1)S(1)}, u32[]{:S(2)}, u32[]{:S(2)}) async-start(bf16[32,8,5]{0,2,1:T(8,128)(2,1)} %copy.122), calls=%async_computation.1 | async-start | bytes 32768 | tf_op jit(solution)/shard_map/all_to_all | solution.py:116
  627.5 434.0 %reduce-scatter.2.cloned.1.call-start = ((), (), s32[]{:S(2)}) async-start(), calls=%async_computation.13 | async-start | bytes 14155776 | tf_op jit(solution)/shard_map/reduce_scatter | solution.py:167
  645.4 6.1 copy-start.6
  651.5 2.9 copy-start.4
  653.0 1.1 copy-start.8
  653.0 1.5 copy-start.10
  698.2 1.3 copy-start.9
  698.2 1.7 copy-start.11
  852.3 96.0 %all-to-all-start.7 = ((bf16[32,8,10240]{2,0,1:T(8,128)(2,1)}), bf16[32,8,10240]{2,0,1:T(8,128)(2,1)}, u32[]{:S(2)}, u32[]{:S(2)}) async-start(bf16[32,8,10240]{2,0,1:T(8,128)(2,1)} %copy.133), calls=%async_computation.7 | async-start | bytes 10485760 | tf_op jit(solution)/shard_map/all_to_all | solution.py:134
  857.4 416.3 %all-reduce.2.cloned.1.call-start = ((), (), s32[]{:S(2)}) async-start(), calls=%async_computation.14 | async-start | bytes 1048576 | tf_op jit(solution)/shard_map/psum | solution.py:185
  977.6 5.2 copy-start.7
  982.8 292.8 %copy-start.1 = (bf16[128,8,1024]{2,1,0:T(8,128)(2,1)S(1)}, bf16[128,8,1024]{2,1,0:T(8,128)(2,1)}, u32[]{:S(2)}) copy-start(bf16[128,8,1024]{2,1,0:T(8,128)(2,1)} %param.9) | copy-start | bytes 6291460
Sparse Core Ops, SparseCore 0:
  698.3 363.1 reduce-scatter.1
Sparse Core Ops, SparseCore 1:
  864.0 409.7 all-reduce.1
where the time goes:
time: 1300 us; the launch traced here: 1280 us
  waiting for transfers between devices  763 us (59%)
  local copies, waits for them, and re-layouts  219 us (17%)
  blocking collectives  157 us (12%)
  starting transfers between devices  59.7 us (5%)
  matrix products  35.6 us (3%)
  other arithmetic  32.2 us (2%)
  between operations  16.7 us (1%)
    psum x1, waiting for transfers between devices, local(): router_grad = lax.psum(local_router, ('expert', 'dp'))  207 us
    all_to_all x1, blocking collectives, local(): lax.all_to_all(part_send, 'expert', split_axis=0, concat_axis=0, tiled=True)  128 us
    all_to_all x1, waiting for transfers between devices, local(): lax.all_to_all(send_grads, 'expert', split_axis=0, concat_axis=0, tiled=T...  115 us
    all_to_all x1, waiting for transfers between devices, local(): lax.all_to_all(send_tokens, 'expert', split_axis=0, concat_axis=0, tiled=...  101 us
    all_to_all x1, waiting for transfers between devices, local(): lax.all_to_all(lax.all_to_all(part_send, 'expert', split_axis=0, concat_a...  89.4 us
    reduce_scatter x1, waiting for transfers between devices, local(): lax.psum_scatter(spread.reshape(row_share * lax.axis_size('dp'), per_grou...  76.7 us
    all_to_all x1, waiting for transfers between devices, local(): lax.all_to_all(lax.all_to_all(send_tokens, 'expert', split_axis=0, concat...  68.2 us
    all_to_all x1, waiting for transfers between devices, local(): lax.all_to_all(lax.all_to_all(send_grads, 'expert', split_axis=0, concat_...  55.2 us
  transfers between devices with their start and end apart: 11, of which 10 were waited for; matrix products, arithmetic and copies ran while one was open for 14% of the time, Pallas kernels for 0%

commit v1 on v0

v1 whole, which is shorter than its diff:
```python
import jax
import jax.numpy as jnp
from jax import lax
from jax.experimental import pallas as pl
from jax.experimental.pallas import tpu as pltpu
from jax.sharding import PartitionSpec as P

zloss_coef = 0.001
balance_coef = 0.01
MESH = pl.DeviceIdType.MESH
ANY = pl.BlockSpec(memory_space=pl.ANY)
BF = jnp.bfloat16
F32 = jnp.float32


def greet(ne, nd, with_expert, with_dp):
    e, d = lax.axis_index("expert"), lax.axis_index("dp")
    barrier = pltpu.get_barrier_semaphore()
    total = 0
    if with_expert:
        def one(i, _):
            pl.semaphore_signal(barrier, inc=1, device_id=(lax.rem(e + i, ne), d), device_id_type=MESH)
            return 0
        lax.fori_loop(1, ne, one, 0)
        total += ne - 1
    if with_dp:
        def two(i, _):
            pl.semaphore_signal(barrier, inc=1, device_id=(e, lax.rem(d + i, nd)), device_id_type=MESH)
            return 0
        lax.fori_loop(1, nd, two, 0)
        total += nd - 1
    pl.semaphore_wait(barrier, total)


def send_all(ne, srcs, dsts, send_sem, recv_sem, local_sem):
    e, d = lax.axis_index("expert"), lax.axis_index("dp")
    for n, (src, dst) in enumerate(zip(srcs, dsts)):
        def one(i, _):
            half = (i + 1) // 2
            odd = lax.rem(i, 2)
            off = odd * half + (1 - odd) * (ne - half)
            peer = lax.rem(e + off, ne)
            pltpu.make_async_remote_copy(
                src_ref=src.at[peer], dst_ref=dst.at[e],
                send_sem=send_sem.at[n], recv_sem=recv_sem.at[n],
                device_id=(peer, d), device_id_type=MESH).start()
            return 0
        lax.fori_loop(1, ne, one, 0)
        pltpu.make_async_copy(src.at[e], dst.at[e], local_sem.at[n]).start()


def wait_all(ne, srcs, dsts, send_sem, recv_sem, local_sem):
    e, d = lax.axis_index("expert"), lax.axis_index("dp")
    for n, (src, dst) in enumerate(zip(srcs, dsts)):
        pltpu.make_async_remote_copy(
            src_ref=src.at[pl.ds(0, ne - 1)], dst_ref=dst.at[pl.ds(0, ne - 1)],
            send_sem=send_sem.at[n], recv_sem=recv_sem.at[n],
            device_id=(lax.rem(e + 1, ne), d), device_id_type=MESH).wait()
        pltpu.make_async_copy(src.at[e], dst.at[e], local_sem.at[n]).wait()


def exchange(arrays, ne, nd, collective_id):
    count = len(arrays)

    def kernel(*refs):
        srcs, dsts = refs[:count], refs[count:2 * count]
        send_sem, recv_sem, local_sem = refs[2 * count:]
        greet(ne, nd, True, False)
        send_all(ne, srcs, dsts, send_sem, recv_sem, local_sem)
        wait_all(ne, srcs, dsts, send_sem, recv_sem, local_sem)

    return pl.pallas_call(
        kernel,
        out_shape=[jax.ShapeDtypeStruct(a.shape, a.dtype) for a in arrays],
        in_specs=[ANY] * count, out_specs=[ANY] * count,
        scratch_shapes=[pltpu.SemaphoreType.DMA((count,))] * 3,
        compiler_params=pltpu.CompilerParams(collective_id=collective_id, has_side_effects=True),
    )(*arrays)


def forward_exchange(arrays, weight, ne, nd, collective_id):
    count = len(arrays)
    width, cols = weight.shape
    rows = width // nd

    def kernel(*refs):
        srcs, w = refs[:count], refs[count]
        dsts, both = refs[count + 1:2 * count + 1], refs[2 * count + 1]
        send_sem, recv_sem, local_sem, root_send, piece_sem, y_sem, x_send, x_recv = refs[2 * count + 2:]
        e, d = lax.axis_index("expert"), lax.axis_index("dp")
        greet(ne, nd, True, True)
        for side, root in ((0, 0), (1, nd - 1)):
            @pl.when(d == root)
            def _():
                pltpu.make_async_copy(
                    w.at[pl.ds(root * rows, rows)], both.at[side, root], piece_sem.at[side]).start()
                for j in [1, 7, 2, 6, 3, 5, 4]:
                    q = (root + j) % nd
                    pltpu.make_async_remote_copy(
                        src_ref=w.at[pl.ds(q * rows, rows)], dst_ref=both.at[side, q],
                        send_sem=root_send.at[side], recv_sem=piece_sem.at[side],
                        device_id=(e, q), device_id_type=MESH).start()
        send_all(ne, srcs[:2], dsts[:2], send_sem, recv_sem, local_sem)
        for side in range(2):
            pltpu.make_async_copy(w.at[pl.ds(0, rows)], both.at[side, d], piece_sem.at[side]).wait()
        pair = d + 1 - 2 * lax.rem(d, 2)
        first = lax.rem(d, 2)
        along_y = pltpu.make_async_remote_copy(
            src_ref=both.at[pl.ds(0, 2), d], dst_ref=both.at[pl.ds(0, 2), d],
            send_sem=y_sem.at[0], recv_sem=y_sem.at[1], device_id=(e, pair), device_id_type=MESH)
        along_y.start()
        send_all_rest = (srcs[2:], dsts[2:], send_sem.at[pl.ds(2, count - 2)], recv_sem.at[pl.ds(2, count - 2)],
                         local_sem.at[pl.ds(2, count - 2)])
        along_y.wait()
        duo = (d // 2) * 2
        copies = []
        for k in (1, 3, 2):
            q = lax.rem(d + 2 * k, nd)
            copies.append(pltpu.make_async_remote_copy(
                src_ref=both.at[pl.ds(0, 2), pl.ds(duo, 2)], dst_ref=both.at[pl.ds(0, 2), pl.ds(duo, 2)],
                send_sem=x_send.at[k - 1], recv_sem=x_recv.at[k - 1], device_id=(e, q), device_id_type=MESH))
        for c in copies:
            c.start()
        send_all(ne, *send_all_rest)
        wait_all(ne, srcs, dsts, send_sem, recv_sem, local_sem)
        for c in copies:
            c.wait()
        for side, root in ((0, 0), (1, nd - 1)):
            @pl.when(d == root)
            def _():
                pltpu.make_async_remote_copy(
                    src_ref=both.at[side, pl.ds(0, nd - 1)], dst_ref=both.at[side, pl.ds(0, nd - 1)],
                    send_sem=root_send.at[side], recv_sem=piece_sem.at[side],
                    device_id=(e, (root + 1) % nd), device_id_type=MESH).wait_send()

    return pl.pallas_call(
        kernel,
        out_shape=[jax.ShapeDtypeStruct(a.shape, a.dtype) for a in arrays]
        + [jax.ShapeDtypeStruct((2, nd, rows, cols), weight.dtype)],
        in_specs=[ANY] * (count + 1), out_specs=[ANY] * (count + 1),
        scratch_shapes=[pltpu.SemaphoreType.DMA((count,))] * 3
        + [pltpu.SemaphoreType.DMA((2,))] * 3 + [pltpu.SemaphoreType.DMA((3,))] * 2,
        compiler_params=pltpu.CompilerParams(collective_id=collective_id, has_side_effects=True),
    )(*arrays, weight)


def backward_exchange(part, grad_up, grad_down, router, ne, nd, collective_id):
    width = grad_up.shape[0]
    two = width // (nd // 2)
    one = width // nd
    cu, cd = grad_up.shape[1], grad_down.shape[1]
    rr, rc = router.shape
    rp = rr // nd
    nchip = ne // 2
    rl = rc // nchip

    def kernel(part, gu, gd, router, back, ou, od, orouter,
               bu, bd, keep_u, keep_d, out_u, out_d, in_u, in_d,
               rbuf, racc, rcore, rmine, rpiece, rfull,
               send_sem, recv_sem, local_sem, a_send, a_recv, own_sem, b_send, b_recv,
               r_send, r_recv, fin_sem):
        e, d = lax.axis_index("expert"), lax.axis_index("dp")
        greet(ne, nd, True, True)

        def rs_dp(i, _):
            q = lax.rem(d + i, nd)
            pltpu.make_async_remote_copy(
                src_ref=router.at[pl.ds(pl.multiple_of(q * rp, rp), rp)], dst_ref=rbuf.at[d],
                send_sem=r_send.at[0], recv_sem=r_recv.at[0], device_id=(e, q), device_id_type=MESH).start()
            return 0
        lax.fori_loop(1, nd, rs_dp, 0)
        own_r = pltpu.make_async_copy(router.at[pl.ds(pl.multiple_of(d * rp, rp), rp)], rbuf.at[d], own_sem.at[2])
        own_r.start()

        x, y = d // 2, lax.rem(d, 2)
        copies = []
        for k in (1, 3, 2):
            xq = lax.rem(x + k, nd // 2)
            src_rows = pl.ds(pl.multiple_of(xq * two, two), two)
            for n, (src, dst) in enumerate(((gu, bu), (gd, bd))):
                copies.append(pltpu.make_async_remote_copy(
                    src_ref=src.at[src_rows], dst_ref=dst.at[k - 1],
                    send_sem=a_send.at[k - 1, n], recv_sem=a_recv.at[k - 1, n],
                    device_id=(e, xq * 2 + y), device_id_type=MESH))
        for c in copies:
            c.start()
        my_rows = pl.ds(pl.multiple_of(x * two, two), two)
        own_u = pltpu.make_async_copy(gu.at[my_rows], bu.at[3], own_sem.at[0])
        own_d = pltpu.make_async_copy(gd.at[my_rows], bd.at[3], own_sem.at[1])
        own_u.start()
        own_d.start()
        send_all(ne, [part], [back], send_sem, recv_sem, local_sem)

        own_r.wait()
        pltpu.make_async_remote_copy(
            src_ref=rbuf.at[pl.ds(0, nd - 1)], dst_ref=rbuf.at[pl.ds(0, nd - 1)],
            send_sem=r_send.at[0], recv_sem=r_recv.at[0], device_id=(e, lax.rem(d + 1, nd)),
            device_id_type=MESH).wait()
        racc[...] = jnp.sum(rbuf[...], axis=0)
        mate = e + 1 - 2 * lax.rem(e, 2)
        core = lax.rem(e, 2)
        chip = e // 2
        cc = pltpu.make_async_remote_copy(
            src_ref=racc, dst_ref=rcore, send_sem=r_send.at[1], recv_sem=r_recv.at[1],
            device_id=(mate, d), device_id_type=MESH)
        cc.start()
        cc.wait()
        for n in range(nchip):
            rmine[n] = racc[:, n * rl:(n + 1) * rl] + rcore[:, n * rl:(n + 1) * rl]

        def rs_chip(i, _):
            q = lax.rem(chip + i, nchip)
            pltpu.make_async_remote_copy(
                src_ref=rmine.at[q], dst_ref=rpiece.at[chip], send_sem=r_send.at[2], recv_sem=r_recv.at[2],
                device_id=(q * 2 + core, d), device_id_type=MESH).start()
            return 0
        lax.fori_loop(1, nchip, rs_chip, 0)
        rpiece[chip] = rmine[chip]
        pltpu.make_async_remote_copy(
            src_ref=rpiece.at[pl.ds(0, nchip - 1)], dst_ref=rpiece.at[pl.ds(0, nchip - 1)],
            send_sem=r_send.at[2], recv_sem=r_recv.at[2], device_id=(mate, d), device_id_type=MESH).wait()
        rfull[chip] = jnp.sum(rpiece[...], axis=0)

        def ag_chip(i, _):
            q = lax.rem(chip + i, nchip)
            pltpu.make_async_remote_copy(
                src_ref=rfull.at[chip], dst_ref=rfull.at[chip], send_sem=r_send.at[3], recv_sem=r_recv.at[3],
                device_id=(q * 2 + core, d), device_id_type=MESH).start()
            return 0
        lax.fori_loop(1, nchip, ag_chip, 0)
        pltpu.make_async_remote_copy(
            src_ref=rfull.at[pl.ds(0, nchip - 1)], dst_ref=rfull.at[pl.ds(0, nchip - 1)],
            send_sem=r_send.at[3], recv_sem=r_recv.at[3], device_id=(mate, d), device_id_type=MESH).wait()

        def ag_dp(i, _):
            q = lax.rem(d + i, nd)
            pltpu.make_async_remote_copy(
                src_ref=rfull, dst_ref=orouter.at[d], send_sem=r_send.at[4], recv_sem=r_recv.at[4],
                device_id=(e, q), device_id_type=MESH).start()
            return 0
        lax.fori_loop(1, nd, ag_dp, 0)
        own_f = pltpu.make_async_copy(rfull, orouter.at[d], own_sem.at[3])
        own_f.start()

        own_u.wait()
        own_d.wait()
        for c in copies:
            c.wait()
        for buf, keep, out in ((bu, keep_u, out_u), (bd, keep_d, out_d)):
            def tile(i, _):
                at = pl.multiple_of(i * 16, 16)
                other = pl.multiple_of((1 - y) * one + i * 16, 16)
                total = buf[0, pl.ds(other, 16), :].astype(F32)
                for n in range(1, 4):
                    total = total + buf[n, pl.ds(other, 16), :].astype(F32)
                out[pl.ds(at, 16), :] = total.astype(BF)
                return 0
            lax.fori_loop(0, one // 16, tile, 0)
        pair = d + 1 - 2 * y
        swaps = []
        for n, (src, dst) in enumerate(((out_u, in_u), (out_d, in_d))):
            c = pltpu.make_async_remote_copy(
                src_ref=src, dst_ref=dst, send_sem=b_send.at[n], recv_sem=b_recv.at[n],
                device_id=(e, pair), device_id_type=MESH)
            c.start()
            swaps.append(c)
        for buf, keep, out in ((bu, keep_u, out_u), (bd, keep_d, out_d)):
            def tile(i, _):
                at = pl.multiple_of(i * 16, 16)
                mine = pl.multiple_of(y * one + i * 16, 16)
                total = buf[0, pl.ds(mine, 16), :].astype(F32)
                for n in range(1, 4):
                    total = total + buf[n, pl.ds(mine, 16), :].astype(F32)
                keep[pl.ds(at, 16), :] = total
                return 0
            lax.fori_loop(0, one // 16, tile, 0)
        for c in swaps:
            c.wait()
        for got, keep, out in ((in_u, keep_u, out_u), (in_d, keep_d, out_d)):
            def tile(i, _):
                at = pl.multiple_of(i * 16, 16)
                out[pl.ds(at, 16), :] = (keep[pl.ds(at, 16), :] + got[pl.ds(at, 16), :].astype(F32)).astype(BF)
                return 0
            lax.fori_loop(0, one // 16, tile, 0)
        f1 = pltpu.make_async_copy(out_u, ou, fin_sem.at[0])
        f2 = pltpu.make_async_copy(out_d, od, fin_sem.at[1])
        f1.start()
        f2.start()
        pltpu.make_async_remote_copy(
            src_ref=orouter.at[pl.ds(0, nd - 1)], dst_ref=orouter.at[pl.ds(0, nd - 1)],
            send_sem=r_send.at[4], recv_sem=r_recv.at[4], device_id=(e, lax.rem(d + 1, nd)),
            device_id_type=MESH).wait()
        own_f.wait()
        wait_all(ne, [part], [back], send_sem, recv_sem, local_sem)
        f1.wait()
        f2.wait()

    dma = pltpu.SemaphoreType.DMA
    return pl.pallas_call(
        kernel,
        out_shape=[jax.ShapeDtypeStruct(part.shape, BF), jax.ShapeDtypeStruct((one, cu), BF),
                   jax.ShapeDtypeStruct((one, cd), BF), jax.ShapeDtypeStruct((nd, nchip, rp, rl), F32)],
        in_specs=[ANY] * 4, out_specs=[ANY] * 4,
        scratch_shapes=[
            pltpu.VMEM((4, two, cu), BF), pltpu.VMEM((4, two, cd), BF),
            pltpu.VMEM((one, cu), F32), pltpu.VMEM((one, cd), F32),
            pltpu.VMEM((one, cu), BF), pltpu.VMEM((one, cd), BF),
            pltpu.VMEM((one, cu), BF), pltpu.VMEM((one, cd), BF),
            pltpu.VMEM((nd, rp, rc), F32), pltpu.VMEM((rp, rc), F32), pltpu.VMEM((rp, rc), F32),
            pltpu.VMEM((nchip, rp, rl), F32), pltpu.VMEM((nchip, rp, rl), F32), pltpu.VMEM((nchip, rp, rl), F32),
            dma((1,)), dma((1,)), dma((1,)), dma((3, 2)), dma((3, 2)), dma((4,)), dma((2,)), dma((2,)),
            dma((5,)), dma((5,)), dma((2,))],
        compiler_params=pltpu.CompilerParams(collective_id=collective_id, has_side_effects=True,
                                             vmem_limit_bytes=48 * 1024 * 1024),
    )(part, grad_up, grad_down, router)


def local(tokens, out_grad, saved_pre, router_weight, slot_expert, slot_of, slot_weight):
    ne = lax.axis_size("expert")
    nd = lax.axis_size("dp")
    rows, width = tokens.shape
    top = slot_of.shape[1]
    half = saved_pre.shape[2] // 2
    experts = router_weight.shape[1]
    slots = slot_expert.shape[0]
    per = rows * top // ne
    total = rows * top

    group = slot_of // nd
    named = group[:, :, None] == jnp.arange(ne, dtype=jnp.int32)[None, None, :]
    names = jnp.sum(named.astype(F32), axis=1)
    before = (lax.broadcasted_iota(jnp.int32, (rows, rows), 1) < lax.broadcasted_iota(jnp.int32, (rows, rows), 0))
    arrival = jnp.dot(before.astype(BF), names.astype(BF), preferred_element_type=F32)
    rank = jnp.sum(jnp.where(named, arrival[:, None, :], 0.0), axis=2).astype(jnp.int32)
    place = (group * per + rank).reshape(-1)
    perm = place[None, :] == lax.broadcasted_iota(jnp.int32, (total, total), 0)
    perm = perm.astype(BF)
    pick = jnp.sum(perm.reshape(total, rows, top).astype(F32), axis=2).astype(BF)

    slot_hot = slot_of[:, :, None] == jnp.arange(slots, dtype=jnp.int32)[None, None, :]
    expert_ids = jnp.sum(jnp.where(slot_hot, slot_expert[None, None, :], 0), axis=2)
    first_expert = jnp.repeat(slot_expert.reshape(ne, nd)[:, 0], nd)
    is_low = jnp.sum(jnp.where(slot_hot, (slot_expert == first_expert).astype(jnp.int32)[None, None, :], 0), axis=2)

    wide_tokens = tokens.astype(F32)
    logits = jnp.dot(wide_tokens, router_weight, precision=lax.Precision.HIGHEST)
    log_total = jax.nn.logsumexp(logits, axis=1)
    router_probs = jnp.exp(logits - log_total[:, None])
    chosen = expert_ids[:, :, None] == jnp.arange(experts, dtype=jnp.int32)[None, None, :]
    chosen_prob = jnp.sum(jnp.where(chosen, router_probs[:, None, :], 0.0), axis=2).astype(BF)
    counts = jnp.sum(chosen.astype(jnp.int32), axis=(0, 1))

    og_send = jnp.dot(pick, out_grad, preferred_element_type=F32).astype(BF).reshape(ne, per, width)
    x_send = jnp.dot(pick, tokens, preferred_element_type=F32).astype(BF).reshape(ne, per, width)
    sv_send = jnp.dot(perm, saved_pre.reshape(total, 2 * half), preferred_element_type=F32).astype(BF)
    sv_send = sv_send.reshape(ne, per, 2 * half)
    facts = jnp.stack([chosen_prob.reshape(-1), is_low.reshape(-1).astype(BF)], axis=1)
    facts = jnp.dot(perm, facts, preferred_element_type=F32).astype(BF).reshape(ne, per, 2)
    facts = jnp.transpose(facts, (0, 2, 1))
    facts = jnp.pad(facts, ((0, 0), (0, 14), (0, 128 - per)))

    og, sv, x, got, both = forward_exchange([og_send, sv_send, x_send, facts], slot_weight[0], ne, nd, 1)
    og, sv, x = og.reshape(total, width), sv.reshape(total, 2 * half), x.reshape(total, width)
    prob = got[:, 0, :per].reshape(total).astype(F32)[:, None]
    low = got[:, 1, :per].reshape(total)[:, None] > 0
    both = both.reshape(2, width, 3 * half)

    gate = sv[:, :half].astype(F32)
    up = sv[:, half:].astype(F32)
    sig = jax.nn.sigmoid(gate)
    active = gate * sig
    hidden = active * up
    back = jnp.where(low, jnp.dot(og, both[0, :, 2 * half:], preferred_element_type=F32),
                     jnp.dot(og, both[1, :, 2 * half:], preferred_element_type=F32))
    prob_grad = jnp.sum(back * hidden, axis=1).astype(BF)
    prob_send = jnp.pad(prob_grad.reshape(ne, 1, per), ((0, 0), (0, 15), (0, 128 - per)))
    (prob_got,) = exchange([prob_send], ne, nd, 2)

    scaled = (prob * hidden).astype(BF)
    hg = prob * back
    pre = jnp.concatenate([hg * up * sig * (1.0 + gate * (1.0 - sig)), hg * active], axis=1).astype(BF)
    zero = jnp.zeros((), BF)
    pre_both = jnp.concatenate([jnp.where(low, pre, zero), jnp.where(low, zero, pre)], axis=1)
    scaled_both = jnp.concatenate([jnp.where(low, scaled, zero), jnp.where(low, zero, scaled)], axis=1)
    contract = (((1,), (1,)), ((), ()))
    part = jnp.where(low, lax.dot_general(pre, both[0, :, :2 * half], contract, preferred_element_type=F32),
                     lax.dot_general(pre, both[1, :, :2 * half], contract, preferred_element_type=F32)).astype(BF)
    grad_up = lax.dot_general(x, pre_both, (((0,), (0,)), ((), ())), preferred_element_type=F32).astype(BF)
    grad_down = lax.dot_general(og, scaled_both, (((0,), (0,)), ((), ())), preferred_element_type=F32).astype(BF)

    prob_row = prob_got[:, 0, :per].reshape(total)
    prob_back = lax.dot_general(perm, prob_row[:, None], (((0,), (0,)), ((), ())), preferred_element_type=F32)
    prob_back = prob_back.reshape(rows, top)
    probs_grad = jnp.sum(jnp.where(chosen, prob_back[:, :, None], 0.0), axis=1)
    probs_grad = probs_grad + balance_coef * experts * counts.astype(F32) / total
    inner = jnp.sum(router_probs * probs_grad, axis=1, keepdims=True)
    logits_grad = router_probs * (probs_grad - inner) + 2.0 * zloss_coef * log_total[:, None] * router_probs
    local_router = lax.dot_general(logits_grad, wide_tokens, (((0,), (0,)), ((), ())),
                                   precision=lax.Precision.HIGHEST)

    part_back, sum_up, sum_down, router_all = backward_exchange(
        part.reshape(ne, per, width), grad_up, grad_down, local_router, ne, nd, 3)
    expert_part = lax.dot_general(pick, part_back.reshape(total, width), (((0,), (0,)), ((), ())),
                                  preferred_element_type=F32)
    router_part = jnp.dot(logits_grad, router_weight.T, precision=lax.Precision.HIGHEST)
    token_grad = (expert_part + router_part).astype(BF)
    router_grad = jnp.transpose(router_all, (0, 2, 1, 3)).reshape(experts, width).T

    low_grad = jnp.concatenate([sum_up[:, :2 * half], sum_down[:, :half]], axis=1)
    high_grad = jnp.concatenate([sum_up[:, 2 * half:], sum_down[:, half:]], axis=1)
    e = lax.axis_index("expert")
    low_first = slot_expert[e * nd] == 2 * e
    expert_grads = jnp.stack([jnp.where(low_first, low_grad, high_grad),
                              jnp.where(low_first, high_grad, low_grad)], axis=1)
    return (token_grad, expert_grads, router_grad)


def solution(mesh):
    placed = (
        P(("expert", "dp"), None),
        P(("expert", "dp"), None),
        P(("expert", "dp"), None, None),
        P(),
        P(),
        P(("expert", "dp"), None),
        P(("expert", "dp"), None, None),
    )
    return jax.shard_map(
        local,
        mesh=mesh,
        in_specs=placed,
        out_specs=(P(("expert", "dp"), None), P("dp", "expert", None), P()),
        check_vma=False,
    )
```

time: 1300 us -> 614 us (0.47)
  waiting for transfers between devices: 763 us -> 0 us
  Pallas kernels: 0 us -> 497 us
  local copies, waits for them, and re-layouts: 219 us -> 15.9 us
  blocking collectives: 157 us -> 0 us
  starting transfers between devices: 59.7 us -> 0 us
  matrix products: 35.6 us -> 73.4 us
  other arithmetic: 32.2 us -> 13.9 us
  between operations: 16.7 us -> 1.79 us
    pallas_call x0 -> x3, Pallas kernels: none -> 497 us  [the longest x1 291 us: forward_exchange(): pl.pallas_call(kernel, out_shape=[jax.ShapeDtypeStruct(a.shape, a.dtype)...]
    all_to_all x9 -> x0, waiting for transfers between devices: 479 us -> none  [the longest x1 115 us: local(): lax.all_to_all(send_grads, 'expert', split_axis=0, concat_axis=0, tiled=T...]
    psum x1 -> x0, waiting for transfers between devices: 207 us -> none  [local(): router_grad = lax.psum(local_router, ('expert', 'dp'))]
    all_to_all x3 -> x0, blocking collectives: 157 us -> none  [the longest x1 128 us: local(): lax.all_to_all(part_send, 'expert', split_axis=0, concat_axis=0, tiled=True)]
    reduce_scatter x1 -> x0, waiting for transfers between devices: 76.7 us -> none  [local(): lax.psum_scatter(spread.reshape(row_share * lax.axis_size('dp'), per_grou...]
    gather x9 -> x0, local copies, waits for them, and re-layouts: 68.4 us -> none  [the longest x2 15.5 us: local(): tokens[owner_row]]
    all_to_all x9 -> x0, starting transfers between devices: 59.7 us -> none  [the longest x1 11.7 us: local(): lax.all_to_all(send_saved, 'expert', split_axis=0, concat_axis=0, tiled=T...]
    all_to_all x11 -> x0, local copies, waits for them, and re-layouts: 53.9 us -> none  [the longest x1 7.72 us: local(): lax.all_to_all(send_tokens, 'expert', split_axis=0, concat_axis=0, tiled=...]
  transfers between devices with their start and end apart: 11 -> 0, of which waited for: 10 -> 0; matrix products, arithmetic and copies ran while one was open for 14% -> 0% of each run, Pallas kernels for 0% -> 0%
where the time goes in v1:
time: 614 us; the launch traced here: 602 us
  Pallas kernels  497 us (81%)
  matrix products  73.4 us (12%)
  local copies, waits for them, and re-layouts  15.9 us (3%)
  other arithmetic  13.9 us (2%)
    pallas_call x1, Pallas kernels, forward_exchange(): pl.pallas_call(kernel, out_shape=[jax.ShapeDtypeStruct(a.shape, a.dtype)...  291 us
    pallas_call x1, Pallas kernels, backward_exchange(): pl.pallas_call(kernel, out_shape=[jax.ShapeDtypeStruct(part.shape, BF), j...  188 us
    pallas_call x1, Pallas kernels, exchange(): pl.pallas_call(kernel, out_shape=[jax.ShapeDtypeStruct(a.shape, a.dtype)...  18.5 us
    dot_general x1, matrix products, local(): lax.dot_general(x, pre_both, (((0,), (0,)), ((), ())), preferred_element_...  12.4 us

profile of v1, /device:TPU:2, one launch (start us, length us, event | category | flops | bytes accessed | tf_op | source)
XLA Modules:
  0.0 602.2 jit_solution(3887252009419298740)
XLA Ops:
  0.6 0.0 copy-start
  0.6 0.8 add_select_fusion
  1.5 0.1 fusion.34
  1.7 0.7 convert_add_fusion
  2.4 1.9 fusion.19
  4.3 4.3 convolution_convert_fusion.2
  8.6 0.1 copy.43
  8.7 0.1 eq.82
  8.8 3.7 fusion.29
  12.5 3.2 convolution_convert_fusion.1
  15.7 0.1 copy.44
  15.8 0.1 reshape.278
  15.9 0.1 slice_reduce_fusion
  16.0 0.1 broadcast_in_dim.135
  16.1 0.1 reshape.279
  16.2 4.6 select_reduce_fusion.1
  20.8 0.1 convert_element_type.128
  20.9 0.7 fusion.46
  21.7 0.5 broadcast_multiply_fusion
  22.3 0.1 select_reduce_fusion.3
  22.3 0.1 copy.46
  22.5 0.1 convert_element_type.125
  22.6 1.3 fusion.33
  23.8 0.1 reshape.280
  23.9 0.7 pad.8.refs_3_
  24.6 290.9 %shard_map.94 = (bf16[32,32,2048]{2,1,0:T(8,128)(2,1)}, bf16[32,32,1024]{2,1,0:T(8,128)(2,1)}, bf16[32,32,2048]{2,1,0:T(8,128)(2,1)}, bf16[32,16,128]{2,1,0:T(8,128)(2,1)}, bf16[2,8,256,1536]{3,2,1,0:T(8,128)(2,1)}) custom-call(bf16[32,32,2048]{2,1,0:T(8,128)(2,1)} %bitcast.73, bf16[32,32,1024]{2,1,0:T(8,128)(2,1)} %bitcast.79, ...), custom_call_target="tpu_custom_call" | custom-call | tf_op jit(solution)/shard_map/pallas_call | solution.py:136
  315.5 2.6 fusion.45
  318.2 0.5 copy.54
  318.7 1.5 copy.55
  320.2 1.5 convert_reduce_fusion.2
  321.7 0.8 reshape.289
  322.5 6.6 %fusion.20 = f32[1024,512]{0,1:T(8,128)} fusion(bf16[1024,2048]{1,0:T(8,128)(2,1)} %bitcast.86, bf16[2,2048,1536]{2,1,0:T(8,128)(2,1)} %bitcast.82), kind=kOutput, calls=%fused_computation.36 | convolution fusion | flops 2147483648 | bytes 8388608 | tf_op jit(solution)/shard_map/dot_general | solution.py:374
  329.1 0.9 compare_reduce_fusion
  330.0 0.1 gt.16
  330.1 7.5 %multiply_reduce_fusion = (bf16[1024]{0:T(1024)(128)(2,1)}, bf16[1024,512]{0,1:T(8,128)(2,1)S(1)}, bf16[1024,512]{0,1:T(8,128)(2,1)S(1)}) fusion(bf16[1024,512]{0,1:T(8,128)(2,1)S(1)} %copy.54, bf16[1024,512]{0,1:T(8,128)(2,1)S(1)} %copy.55, f32[1024]{0:T(1024)S(1)} %reshape.289, f32[1024,512]{0,1:T(8,128)} %fusion.20, bf16[1024,2048]{1,0:T(8,128)(2,1)} %bitcast.87, ...), kind=kOutput, calls=%fused_computation.44 | convolution fusion | flops 2157968384 | bytes 12590080 | tf_op jit(solution)/shard_map/dot_general | solution.py:373
  337.6 7.0 %fusion = bf16[1024,2048]{1,0:T(8,128)(2,1)S(1)} fusion(bf16[2,2048,1536]{2,1,0:T(8,128)(2,1)} %bitcast.84, bf16[1024,512]{0,1:T(8,128)(2,1)S(1)} %get-tuple-element.41, bf16[1024,512]{0,1:T(8,128)(2,1)S(1)} %get-tuple-element.40), kind=kOutput, calls=%fused_computation.3 | convolution fusion | flops 4299161600 | bytes 10485760 | tf_op jit(solution)/shard_map/dot_general | solution.py:387
  344.6 9.4 %select_convert_fusion = bf16[1024,2048]{1,0:T(8,128)(2,1)} fusion(bf16[1024,2048]{1,0:T(8,128)(2,1)S(1)} %fusion, pred[1024]{0:T(1024)(128)(4,1)S(1)} %gt.16, bf16[2,2048,1536]{2,1,0:T(8,128)(2,1)} %bitcast.85, bf16[1024,512]{0,1:T(8,128)(2,1)S(1)} %get-tuple-element.41, bf16[1024,512]{0,1:T(8,128)(2,1)S(1)} %get-tuple-element.40), kind=kOutput, calls=%fused_computation | convolution fusion | flops 4301258752 | bytes 14681088 | tf_op jit(solution)/shard_map/dot_general | solution.py:386
  354.0 1.0 broadcast_select_fusion.1
  355.0 1.2 copy-done.12
  356.2 12.4 %convolution_convert_fusion.gu = bf16[2048,2048]{1,0:T(8,128)(2,1)} fusion(bf16[1024,2048]{1,0:T(8,128)(2,1)S(1)} %bitcast.89, bf16[1024,1024]{0,1:T(8,128)(2,1)S(1)} %get-tuple-element.43, bf16[1024,1024]{0,1:T(8,128)(2,1)S(1)} %get-tuple-element.42), kind=kOutput, calls=%fused_computation.1 | convolution fusion | flops 8602517504 | bytes 16777216 | tf_op jit(solution)/shard_map/dot_general | solution.py:388
  368.6 0.9 broadcast_select_fusion.3
  369.5 0.1 broadcast_select_fusion.2
  369.6 1.2 copy-done.11
  370.8 7.3 %convolution_convert_fusion.3.gd = bf16[2048,1024]{1,0:T(8,128)(2,1)} fusion(bf16[1024,2048]{1,0:T(8,128)(2,1)S(1)} %bitcast.88, bf16[1024,512]{0,1:T(8,128)(2,1)S(1)} %broadcast_select_fusion.2, bf16[1024,512]{0,1:T(8,128)(2,1)S(1)} %get-tuple-element.37), kind=kOutput, calls=%fused_computation.19 | convolution fusion | flops 4301258752 | bytes 10485760 | tf_op jit(solution)/shard_map/dot_general | solution.py:389
  378.1 0.1 convert_element_type.144
  378.2 0.7 pad.9.refs_0_
  378.8 18.5 %shard_map.95 = bf16[32,16,128]{2,1,0:T(8,128)(2,1)} custom-call(bf16[32,16,128]{2,1,0:T(8,128)(2,1)} %pad.9.refs_0_), custom_call_target="tpu_custom_call" | custom-call | tf_op jit(solution)/shard_map/pallas_call | solution.py:72
  397.3 0.9 slice_reduce_fusion.1
  398.2 0.1 reshape.290
  398.3 4.8 fusion.9
  403.1 0.1 copy.53
  403.1 0.1 select_reduce_fusion.2
  403.2 0.1 convert_reduce_fusion
  403.4 0.1 multiply_reduce_fusion.1
  403.5 0.4 fusion.41.router
  403.9 187.8 %shard_map.96 = (bf16[32,32,2048]{2,1,0:T(8,128)(2,1)}, bf16[256,2048]{1,0:T(8,128)(2,1)S(1)}, bf16[256,1024]{1,0:T(8,128)(2,1)S(1)}, f32[8,16,8,128]{3,2,1,0:T(8,128)S(1)}) custom-call(bf16[32,32,2048]{2,1,0:T(8,128)(2,1)} %bitcast.77, bf16[2048,2048]{1,0:T(8,128)(2,1)} %convolution_convert_fusion.gu, bf16[2048,1024]{1,0:T(8,128)(2,1)} %convolution_convert_fusion.3.gd, ...), custom_call_target="tpu_custom_call" | custom-call | tf_op jit(solution)/shard_map/pallas_call | solution.py:299
  591.7 2.9 fusion.47
  594.6 1.9 fusion.11
  596.5 0.6 dynamic_slice.3
  597.8 0.1 slice_bitcast_fusion.13
  597.9 0.3 broadcast_select_fusion.5
  598.2 0.1 pad_maximum_fusion.1
  598.4 2.8 copy.52
  601.1 0.8 copy.59
  (34 shorter events, 0.3 us)
Async XLA Ops:
  0.6 8.2 %copy-start = (bf16[128,8,1024]{2,1,0:T(8,128)(2,1)S(1)}, bf16[128,8,1024]{2,1,0:T(8,128)(2,1)}, u32[]{:S(2)}) copy-start(bf16[128,8,1024]{2,1,0:T(8,128)(2,1)} %param.9) | copy-start | bytes 6291460
  8.8 3.7 copy-start.2
  12.5 3.2 copy-start.4
  12.5 3.3 copy-start.5
  12.5 8.4 %copy-start.3 = (f32[2048,64]{0,1:T(8,128)S(1)}, f32[2048,64]{0,1:T(8,128)}, u32[]{:S(2)}) copy-start(f32[2048,64]{0,1:T(8,128)} %param.10) | copy-start | bytes 1572868
  22.2 293.3 %copy-start.8 = (f32[128]{0:T(128)}, f32[128]{0:T(128)S(1)}, u32[]{:S(2)}) copy-start(f32[128]{0:T(128)S(1)} %get-tuple-element.36) | copy-start | bytes 1540
  354.0 2.2 copy-start.12
  368.6 2.2 copy-start.11
  370.8 7.3 %copy-start.10 = (bf16[1024]{0:T(1024)(128)(2,1)S(1)}, bf16[1024]{0:T(1024)(128)(2,1)}, u32[]{:S(2)}) copy-start(bf16[1024]{0:T(1024)(128)(2,1)} %get-tuple-element.39) | copy-start | bytes 6148
  378.1 25.3 %copy-start.9 = (f32[128]{0:T(128)S(1)}, f32[128]{0:T(128)}, u32[]{:S(2)}) copy-start(f32[128]{0:T(128)} %copy-done.8) | copy-start | bytes 1540
  378.1 25.4 %copy-start.7 = (f32[128]{0:T(128)S(1)}, f32[128]{0:T(128)}, u32[]{:S(2)}) copy-start(f32[128]{0:T(128)} %get-tuple-element.35) | copy-start | bytes 1540
  594.6 1.9 copy-start.6
  598.2 3.7 copy-start.1

commit v2 on v1

v2 whole, which is shorter than its diff:
```python
import jax
import jax.numpy as jnp
from jax import lax
from jax.experimental import pallas as pl
from jax.experimental.pallas import tpu as pltpu
from jax.sharding import PartitionSpec as P

zloss_coef = 0.001
balance_coef = 0.01
MESH = pl.DeviceIdType.MESH
ANY = pl.BlockSpec(memory_space=pl.ANY)
BF = jnp.bfloat16
F32 = jnp.float32


def greet(ne, nd, with_expert, with_dp):
    e, d = lax.axis_index("expert"), lax.axis_index("dp")
    barrier = pltpu.get_barrier_semaphore()
    total = 0
    if with_expert:
        def one(i, _):
            pl.semaphore_signal(barrier, inc=1, device_id=(lax.rem(e + i, ne), d), device_id_type=MESH)
            return 0
        lax.fori_loop(1, ne, one, 0)
        total += ne - 1
    if with_dp:
        def two(i, _):
            pl.semaphore_signal(barrier, inc=1, device_id=(e, lax.rem(d + i, nd)), device_id_type=MESH)
            return 0
        lax.fori_loop(1, nd, two, 0)
        total += nd - 1
    pl.semaphore_wait(barrier, total)


def send_all(ne, srcs, dsts, send_sem, recv_sem, local_sem):
    e, d = lax.axis_index("expert"), lax.axis_index("dp")
    for n, (src, dst) in enumerate(zip(srcs, dsts)):
        def one(i, _):
            half = (i + 1) // 2
            odd = lax.rem(i, 2)
            off = odd * half + (1 - odd) * (ne - half)
            peer = lax.rem(e + off, ne)
            pltpu.make_async_remote_copy(
                src_ref=src.at[peer], dst_ref=dst.at[e],
                send_sem=send_sem.at[n], recv_sem=recv_sem.at[n],
                device_id=(peer, d), device_id_type=MESH).start()
            return 0
        lax.fori_loop(1, ne, one, 0)
        pltpu.make_async_copy(src.at[e], dst.at[e], local_sem.at[n]).start()


def wait_all(ne, srcs, dsts, send_sem, recv_sem, local_sem):
    e, d = lax.axis_index("expert"), lax.axis_index("dp")
    for n, (src, dst) in enumerate(zip(srcs, dsts)):
        pltpu.make_async_remote_copy(
            src_ref=src.at[pl.ds(0, ne - 1)], dst_ref=dst.at[pl.ds(0, ne - 1)],
            send_sem=send_sem.at[n], recv_sem=recv_sem.at[n],
            device_id=(lax.rem(e + 1, ne), d), device_id_type=MESH).wait()
        pltpu.make_async_copy(src.at[e], dst.at[e], local_sem.at[n]).wait()


def forward_exchange(tokens, out_grad, saved, facts, pick, weight, ne, nd, collective_id):
    rows, width = tokens.shape
    nz = pick.shape[0]
    nq = ne // nz
    per = saved.shape[1]
    cols = weight.shape[1]
    wr = width // nd
    nc = 3
    cw = cols // nc
    tile = 512
    hops = nz // 2

    def kernel(tok, og, sv, fa, pk, w, og_r, x_r, sv_r, fa_r, both,
               ring, picked, hot,
               in_sem, pk_sem, ring_send, ring_recv, sel_send, sel_recv, sel_local,
               send_sem, recv_sem, local_sem, root_send, piece_sem, y_send, y_recv,
               x_send, x_recv, r_send, r_recv):
        e, d = lax.axis_index("expert"), lax.axis_index("dp")
        core = lax.rem(e, 2)
        z = lax.rem(e // 2, nz)
        hi = e // (2 * nz)
        quarter = hi * 2 + core

        def at(zz):
            return hi * (2 * nz) + zz * 2 + core

        loads = [pltpu.make_async_copy(og, ring.at[0, z], in_sem.at[0]),
                 pltpu.make_async_copy(tok, ring.at[1, z], in_sem.at[1]),
                 pltpu.make_async_copy(pk.at[z], hot.at[z], in_sem.at[2])]
        for c in loads:
            c.start()
        greet(ne, nd, True, True)

        order = (2, 0, 1)
        for side, root in ((0, 0), (1, nd - 1)):
            @pl.when(d == root)
            def _():
                for c in order:
                    span = pl.ds(c * cw, cw)
                    pltpu.make_async_copy(
                        w.at[pl.ds(root * wr, wr), span], both.at[side, root, :, span], piece_sem.at[side, c]).start()
                    for j in [1, 7, 2, 6, 3, 5, 4]:
                        q = (root + j) % nd
                        pltpu.make_async_remote_copy(
                            src_ref=w.at[pl.ds(q * wr, wr), span], dst_ref=both.at[side, q, :, span],
                            send_sem=root_send.at[side], recv_sem=piece_sem.at[side, c],
                            device_id=(e, q), device_id_type=MESH).start()

        def hot_send(i, _):
            q = lax.rem(z + i, nz)
            pltpu.make_async_remote_copy(
                src_ref=pk.at[q], dst_ref=hot.at[z], send_sem=pk_sem.at[0], recv_sem=pk_sem.at[1],
                device_id=(at(q), d), device_id_type=MESH).start()
            return 0
        lax.fori_loop(1, nz, hot_send, 0)

        def ring_copy(n, direction, step):
            sign = 1 - 2 * direction
            block = lax.rem(z - sign * step + nz, nz)
            to = lax.rem(z + sign + nz, nz)
            part = pl.ds(0, rows) if step < hops - 1 else pl.ds(direction * (rows // 2), rows // 2)
            return pltpu.make_async_remote_copy(
                src_ref=ring.at[n, block, part], dst_ref=ring.at[n, block, part],
                send_sem=ring_send.at[n, direction, step], recv_sem=ring_recv.at[n, direction, step],
                device_id=(at(to), d), device_id_type=MESH)

        copies = {(n, g, s): ring_copy(n, g, s) for n in range(2) for g in range(2) for s in range(hops)}
        for n in range(2):
            loads[n].wait()
            for g in range(2):
                copies[n, g, 0].start()
        send_all(ne, [sv, fa], [sv_r, fa_r], send_sem, recv_sem, local_sem)

        loads[2].wait()
        pltpu.make_async_remote_copy(
            src_ref=pk.at[pl.ds(0, nz - 1)], dst_ref=hot.at[pl.ds(0, nz - 1)],
            send_sem=pk_sem.at[0], recv_sem=pk_sem.at[1], device_id=(at(lax.rem(z + 1, nz)), d),
            device_id_type=MESH).wait()
        outs = (og_r, x_r)

        def choose(n, block):
            def one(i, _):
                span = pl.ds(pl.multiple_of(i * tile, tile), tile)
                picked[n, block, :, span] = jnp.dot(
                    hot[block], ring[n, block, :, span], preferred_element_type=F32).astype(BF)
                return 0
            lax.fori_loop(0, width // tile, one, 0)
            src_index = at(block)

            def hand(i, _):
                q = lax.rem(quarter + i, nq)
                pltpu.make_async_remote_copy(
                    src_ref=picked.at[n, block, pl.ds(pl.multiple_of(q * per, per), per)],
                    dst_ref=outs[n].at[src_index], send_sem=sel_send.at[n], recv_sem=sel_recv.at[n],
                    device_id=((q // 2) * (2 * nz) + z * 2 + lax.rem(q, 2), d), device_id_type=MESH).start()
                return 0
            lax.fori_loop(1, nq, hand, 0)
            pltpu.make_async_copy(
                picked.at[n, block, pl.ds(pl.multiple_of(quarter * per, per), per)],
                outs[n].at[src_index], sel_local.at[n]).start()

        pair = d + 1 - 2 * lax.rem(d, 2)
        x, y = d // 2, lax.rem(d, 2)
        nx = nd // 2

        def scattered(c):
            span = pl.ds(c * cw, cw)
            for side in range(2):
                pltpu.make_async_copy(
                    w.at[pl.ds(0, wr), span], both.at[side, d, :, span], piece_sem.at[side, c]).wait()

        def along_y(c):
            part = both.at[pl.ds(0, 2), d, :, pl.ds(c * cw, cw)]
            return pltpu.make_async_remote_copy(
                src_ref=part, dst_ref=part, send_sem=y_send.at[c], recv_sem=y_recv.at[c],
                device_id=(e, pair), device_id_type=MESH)

        def along_x(c, g):
            part = both.at[pl.ds(0, 2), pl.ds(x * 2, 2), :, pl.ds(c * cw, cw)]
            to = lax.rem(x + 1 + 2 * g, nx)
            return pltpu.make_async_remote_copy(
                src_ref=part, dst_ref=part, send_sem=x_send.at[c, g], recv_sem=x_recv.at[c, g],
                device_id=(e, to * 2 + y), device_id_type=MESH)

        def relay(c, g):
            source = lax.rem(x + 3 - 2 * g, nx)
            part = both.at[g, pl.ds(source * 2, 2), :, pl.ds(c * cw, cw)]
            to = lax.rem(x + 1 + 2 * g, nx)
            return pltpu.make_async_remote_copy(
                src_ref=part, dst_ref=part, send_sem=r_send.at[c, g], recv_sem=r_recv.at[c, g],
                device_id=(e, to * 2 + y), device_id_type=MESH)

        ys = {c: along_y(c) for c in order}
        xs = {(c, g): along_x(c, g) for c in order for g in range(2)}
        rs = {(c, g): relay(c, g) for c in order for g in range(2)}

        def stage_y(c):
            scattered(c)
            ys[c].start()

        def stage_x(c):
            ys[c].wait()
            for g in range(2):
                xs[c, g].start()

        def stage_r(c):
            for g in range(2):
                xs[c, g].wait()
                rs[c, g].start()

        def ring_step(s):
            for n in range(2):
                for g in range(2):
                    copies[n, g, s].wait()
                    if s + 1 < hops:
                        copies[n, g, s + 1].start()
            for n in range(2):
                choose(n, lax.rem(z + nz - s - 1, nz))
                if s + 1 < hops:
                    choose(n, lax.rem(z + s + 1, nz))

        for n in range(2):
            choose(n, z)
        stage_y(order[0])
        stage_x(order[0])
        ring_step(0)
        stage_y(order[1])
        stage_x(order[1])
        stage_r(order[0])
        ring_step(1)
        stage_y(order[2])
        stage_x(order[2])
        stage_r(order[1])
        ring_step(2)
        stage_r(order[2])
        ring_step(3)
        for c in order:
            for g in range(2):
                rs[c, g].wait()
        wait_all(ne, [sv, fa], [sv_r, fa_r], send_sem, recv_sem, local_sem)
        for n in range(2):
            far = nz * (nq - 1)
            pltpu.make_async_remote_copy(
                src_ref=outs[n].at[pl.ds(0, far)], dst_ref=outs[n].at[pl.ds(0, far)],
                send_sem=sel_send.at[n], recv_sem=sel_recv.at[n], device_id=(at(lax.rem(z + 1, nz)), d),
                device_id_type=MESH).wait()
            pltpu.make_async_copy(
                outs[n].at[pl.ds(0, nz)], outs[n].at[pl.ds(0, nz)], sel_local.at[n]).wait()
        for side, root in ((0, 0), (1, nd - 1)):
            @pl.when(d == root)
            def _():
                pltpu.make_async_remote_copy(
                    src_ref=both.at[side, pl.ds(0, nd - 1)], dst_ref=both.at[side, pl.ds(0, nd - 1)],
                    send_sem=root_send.at[side], recv_sem=piece_sem.at[side, 0],
                    device_id=(e, (root + 1) % nd), device_id_type=MESH).wait_send()

    dma = pltpu.SemaphoreType.DMA
    shape = jax.ShapeDtypeStruct
    return pl.pallas_call(
        kernel,
        out_shape=[shape((ne, per, width), BF), shape((ne, per, width), BF), shape(saved.shape, BF),
                   shape(facts.shape, BF), shape((2, nd, wr, cols), BF)],
        in_specs=[ANY] * 6, out_specs=[ANY] * 5,
        scratch_shapes=[
            pltpu.VMEM((2, nz, rows, width), BF), pltpu.VMEM((2, nz, rows, width), BF),
            pltpu.VMEM((nz, nq * per, rows), BF),
            dma((3,)), dma((2,)), dma((2, 2, hops)), dma((2, 2, hops)), dma((2,)), dma((2,)), dma((2,)),
            dma((2,)), dma((2,)), dma((2,)), dma((2,)), dma((2, nc)), dma((nc,)), dma((nc,)),
            dma((nc, 2)), dma((nc, 2)), dma((nc, 2)), dma((nc, 2))],
        compiler_params=pltpu.CompilerParams(collective_id=collective_id, has_side_effects=True,
                                             vmem_limit_bytes=40 * 1024 * 1024),
    )(tokens, out_grad, saved, facts, pick, weight)


def backward_exchange(x_rows, og_rows, pre, scaled, both, prob, hot_expert, hot_token, probs, base, extra, tokens,
                      ne, nd, collective_id):
    total, width = x_rows.shape
    per = total // ne
    nx = nd // 2
    two = width // nx
    one = width // nd
    cw = scaled.shape[1]
    rows = tokens.shape[0]
    experts = 2 * ne
    rp = experts // nd
    nchip = ne // 2
    rl = width // nchip
    nc = 3
    st = 32

    def kernel(xr, ogr, pr, sc, wb, qr, he, ht, pb, ba, ex, tk, back, ow, orouter, olg,
               xv, ov, pv, sv, wv, qv, hev, htv, pbv, bav, exv, tkv, lg, partv,
               far, near, own, got_half, got_full, yout, yin,
               rpart, rbuf, racc, rcore, rmine, rpiece, rfull,
               in_sem, q_sem, q_local, send_sem, recv_sem, local_sem,
               a_send, a_recv, b_send, b_recv, y_send, y_recv, r_send, r_recv, misc, fin_sem):
        e, d = lax.axis_index("expert"), lax.axis_index("dp")
        x, y = d // 2, lax.rem(d, 2)
        plus, minus, across = lax.rem(x + 1, nx), lax.rem(x + 3, nx), lax.rem(x + 2, nx)
        pairs = [(ogr, ov), (sc, sv), (xr, xv), (pr, pv), (he, hev), (ht, htv), (pb, pbv), (ba, bav), (ex, exv),
                 (tk, tkv), (wb.at[pl.ds(0, 2), pl.ds(0, nd), :, pl.ds(0, cw)], wv)]
        loads = [pltpu.make_async_copy(s, t, in_sem.at[n]) for n, (s, t) in enumerate(pairs)]
        for c in loads:
            c.start()
        greet(ne, nd, True, True)
        send_all(ne, [qr], [qv], q_sem.at[pl.ds(0, 1)], q_sem.at[pl.ds(1, 1)], q_local)

        def operand(c):
            if c == 0:
                return ov, sv, 0
            return xv, pv, (c - 1) * cw

        def contribute(c, target, out):
            left, right, at = operand(c)

            def half(i, _):
                from_row = pl.multiple_of(target * two + i * one, one)
                out[pl.ds(pl.multiple_of(i * one, one), one), :] = lax.dot_general(
                    left[:, pl.ds(from_row, one)], right[:, pl.ds(at, cw)], (((0,), (0,)), ((), ())),
                    preferred_element_type=F32).astype(BF)
                return 0
            lax.fori_loop(0, 2, half, 0)

        def first(c, g):
            return pltpu.make_async_remote_copy(
                src_ref=far.at[c, pl.ds(g * one, one)], dst_ref=got_half.at[c, g],
                send_sem=a_send.at[c, g], recv_sem=a_recv.at[c, g],
                device_id=(e, (plus if g == 0 else minus) * 2 + y), device_id_type=MESH)

        def second(c, g):
            return pltpu.make_async_remote_copy(
                src_ref=near.at[c, g], dst_ref=got_full.at[c, g],
                send_sem=b_send.at[c, g], recv_sem=b_recv.at[c, g],
                device_id=(e, (plus if g == 0 else minus) * 2 + y), device_id_type=MESH)

        def swap(c):
            return pltpu.make_async_remote_copy(
                src_ref=yout.at[c], dst_ref=yin.at[c], send_sem=y_send.at[c], recv_sem=y_recv.at[c],
                device_id=(e, d + 1 - 2 * y), device_id_type=MESH)

        firsts = {(c, g): first(c, g) for c in range(nc) for g in range(2)}
        seconds = {(c, g): second(c, g) for c in range(nc) for g in range(2)}
        swaps = [swap(c) for c in range(nc)]

        def start_far(c):
            contribute(c, across, far.at[c])
            for g in range(2):
                firsts[c, g].start()

        def start_near(c):
            for g in range(2):
                firsts[c, g].wait()

                def add(i, _):
                    src = pl.ds(pl.multiple_of(i * st, st), st)
                    dst = pl.ds(pl.multiple_of(g * one + i * st, st), st)
                    near[c, g, dst, :] = (near[c, g, dst, :].astype(F32)
                                          + got_half[c, g, src, :].astype(F32)).astype(BF)
                    return 0
                lax.fori_loop(0, one // st, add, 0)
                seconds[c, g].start()

        def start_swap(c):
            for g in range(2):
                seconds[c, g].wait()

            def add(i, _):
                src = pl.ds(pl.multiple_of((1 - y) * one + i * st, st), st)
                yout[c, pl.ds(pl.multiple_of(i * st, st), st), :] = (
                    own[c, src, :].astype(F32) + got_full[c, 0, src, :].astype(F32)
                    + got_full[c, 1, src, :].astype(F32)).astype(BF)
                return 0
            lax.fori_loop(0, one // st, add, 0)
            swaps[c].start()

        def finish(c):
            swaps[c].wait()

            def add(i, _):
                src = pl.ds(pl.multiple_of(y * one + i * st, st), st)
                at = pl.ds(pl.multiple_of(i * st, st), st)
                yout[c, at, :] = (
                    own[c, src, :].astype(F32) + got_full[c, 0, src, :].astype(F32)
                    + got_full[c, 1, src, :].astype(F32) + yin[c, at, :].astype(F32)).astype(BF)
                return 0
            lax.fori_loop(0, one // st, add, 0)
            pltpu.make_async_copy(yout.at[c], ow.at[c], fin_sem.at[c]).start()

        loads[0].wait()
        loads[1].wait()
        start_far(0)
        loads[2].wait()
        loads[3].wait()
        start_far(1)
        start_far(2)

        for n in range(4, 10):
            loads[n].wait()
        wait_all(ne, [qr], [qv], q_sem.at[pl.ds(0, 1)], q_sem.at[pl.ds(1, 1)], q_local)
        chosen = hev[...] * qv[...].reshape(total, 128)
        grad = jnp.dot(htv[...], chosen, preferred_element_type=F32) + bav[...]
        inner = jnp.sum(pbv[...] * grad, axis=1, keepdims=True)
        grad = pbv[...] * (grad - inner) + exv[...]
        lg[...] = grad
        lg_out = pltpu.make_async_copy(lg, olg, misc.at[3])
        lg_out.start()
        turned = grad.T[:experts]
        high = turned.astype(BF)
        rest = turned - high.astype(F32)
        middle = rest.astype(BF)
        low = (rest - middle.astype(F32)).astype(BF)

        def router_tile(i, _):
            span = pl.ds(pl.multiple_of(i * 512, 512), 512)
            t = tkv[:, span]
            rpart[:, span] = (jnp.dot(low, t, preferred_element_type=F32)
                              + jnp.dot(middle, t, preferred_element_type=F32)
                              + jnp.dot(high, t, preferred_element_type=F32))
            return 0
        lax.fori_loop(0, width // 512, router_tile, 0)

        def rs_dp(i, _):
            q = lax.rem(d + i, nd)
            pltpu.make_async_remote_copy(
                src_ref=rpart.at[pl.ds(pl.multiple_of(q * rp, rp), rp)], dst_ref=rbuf.at[d],
                send_sem=r_send.at[0], recv_sem=r_recv.at[0], device_id=(e, q), device_id_type=MESH).start()
            return 0
        lax.fori_loop(1, nd, rs_dp, 0)
        rbuf[d] = rpart[pl.ds(pl.multiple_of(d * rp, rp), rp), :]

        contribute(0, plus, near.at[0, 0])
        contribute(0, minus, near.at[0, 1])

        pltpu.make_async_remote_copy(
            src_ref=rbuf.at[pl.ds(0, nd - 1)], dst_ref=rbuf.at[pl.ds(0, nd - 1)],
            send_sem=r_send.at[0], recv_sem=r_recv.at[0], device_id=(e, lax.rem(d + 1, nd)),
            device_id_type=MESH).wait()
        racc[...] = jnp.sum(rbuf[...], axis=0)
        mate = e + 1 - 2 * lax.rem(e, 2)
        core = lax.rem(e, 2)
        chip = e // 2
        cc = pltpu.make_async_remote_copy(
            src_ref=racc, dst_ref=rcore, send_sem=r_send.at[1], recv_sem=r_recv.at[1],
            device_id=(mate, d), device_id_type=MESH)
        cc.start()

        start_near(0)
        contribute(1, plus, near.at[1, 0])
        contribute(1, minus, near.at[1, 1])

        cc.wait()
        for n in range(nchip):
            rmine[n] = racc[:, n * rl:(n + 1) * rl] + rcore[:, n * rl:(n + 1) * rl]

        def rs_chip(i, _):
            q = lax.rem(chip + i, nchip)
            pltpu.make_async_remote_copy(
                src_ref=rmine.at[q], dst_ref=rpiece.at[chip], send_sem=r_send.at[2], recv_sem=r_recv.at[2],
                device_id=(q * 2 + core, d), device_id_type=MESH).start()
            return 0
        lax.fori_loop(1, nchip, rs_chip, 0)
        rpiece[chip] = rmine[chip]

        loads[10].wait()

        def part_tile(i, _):
            j, r = i // 4, lax.rem(i, 4)
            at = pl.ds(pl.multiple_of(r * (total // 4), total // 4), total // 4)
            contract = (((1,), (1,)), ((), ()))
            value = lax.dot_general(pv[at, :cw], wv[0, j], contract, preferred_element_type=F32)
            value = value + lax.dot_general(pv[at, cw:], wv[1, j], contract, preferred_element_type=F32)
            span = pl.ds(pl.multiple_of(j * one, one), one)
            partv[pl.ds(r * (ne // 4), ne // 4), :, span] = value.astype(BF).reshape(ne // 4, per, one)
            return 0
        lax.fori_loop(0, 4 * nd, part_tile, 0)
        send_all(ne, [partv], [back], send_sem, recv_sem, local_sem)

        start_near(1)
        pltpu.make_async_remote_copy(
            src_ref=rpiece.at[pl.ds(0, nchip - 1)], dst_ref=rpiece.at[pl.ds(0, nchip - 1)],
            send_sem=r_send.at[2], recv_sem=r_recv.at[2], device_id=(mate, d), device_id_type=MESH).wait()
        rfull[chip] = jnp.sum(rpiece[...], axis=0)

        def ag_chip(i, _):
            q = lax.rem(chip + i, nchip)
            pltpu.make_async_remote_copy(
                src_ref=rfull.at[chip], dst_ref=rfull.at[chip], send_sem=r_send.at[3], recv_sem=r_recv.at[3],
                device_id=(q * 2 + core, d), device_id_type=MESH).start()
            return 0
        lax.fori_loop(1, nchip, ag_chip, 0)

        contribute(2, plus, near.at[2, 0])
        contribute(2, minus, near.at[2, 1])
        start_near(2)
        for c in range(nc):
            contribute(c, x, own.at[c])

        pltpu.make_async_remote_copy(
            src_ref=rfull.at[pl.ds(0, nchip - 1)], dst_ref=rfull.at[pl.ds(0, nchip - 1)],
            send_sem=r_send.at[3], recv_sem=r_recv.at[3], device_id=(mate, d), device_id_type=MESH).wait()

        def ag_dp(i, _):
            q = lax.rem(d + i, nd)
            pltpu.make_async_remote_copy(
                src_ref=rfull, dst_ref=orouter.at[d], send_sem=r_send.at[4], recv_sem=r_recv.at[4],
                device_id=(e, q), device_id_type=MESH).start()
            return 0
        lax.fori_loop(1, nd, ag_dp, 0)
        own_f = pltpu.make_async_copy(rfull, orouter.at[d], misc.at[0])
        own_f.start()

        start_swap(0)
        start_swap(1)
        finish(0)
        start_swap(2)
        finish(1)
        finish(2)

        pltpu.make_async_remote_copy(
            src_ref=orouter.at[pl.ds(0, nd - 1)], dst_ref=orouter.at[pl.ds(0, nd - 1)],
            send_sem=r_send.at[4], recv_sem=r_recv.at[4], device_id=(e, lax.rem(d + 1, nd)),
            device_id_type=MESH).wait()
        own_f.wait()
        lg_out.wait()
        wait_all(ne, [partv], [back], send_sem, recv_sem, local_sem)
        for c in range(nc):
            pltpu.make_async_copy(yout.at[c], ow.at[c], fin_sem.at[c]).wait()

    dma = pltpu.SemaphoreType.DMA
    shape = jax.ShapeDtypeStruct
    vmem = pltpu.VMEM
    return pl.pallas_call(
        kernel,
        out_shape=[shape((ne, per, width), BF), shape((nc, one, cw), BF), shape((nd, nchip, rp, rl), F32),
                   shape((rows, 128), F32)],
        in_specs=[ANY] * 12, out_specs=[ANY] * 4,
        scratch_shapes=[
            vmem((total, width), BF), vmem((total, width), BF), vmem((total, 2 * cw), BF), vmem((total, cw), BF),
            vmem((2, nd, one, cw), BF), vmem((ne, per, 128), BF), vmem((total, 128), BF), vmem((rows, total), BF),
            vmem((rows, 128), F32), vmem((1, 128), F32), vmem((rows, 128), F32), vmem((rows, width), BF),
            vmem((rows, 128), F32), vmem((ne, per, width), BF),
            vmem((nc, two, cw), BF), vmem((nc, 2, two, cw), BF), vmem((nc, two, cw), BF),
            vmem((nc, 2, one, cw), BF), vmem((nc, 2, two, cw), BF), vmem((nc, one, cw), BF), vmem((nc, one, cw), BF),
            vmem((experts, width), F32), vmem((nd, rp, width), F32), vmem((rp, width), F32), vmem((rp, width), F32),
            vmem((nchip, rp, rl), F32), vmem((nchip, rp, rl), F32), vmem((nchip, rp, rl), F32),
            dma((11,)), dma((2,)), dma((1,)), dma((1,)), dma((1,)), dma((1,)),
            dma((nc, 2)), dma((nc, 2)), dma((nc, 2)), dma((nc, 2)), dma((nc,)), dma((nc,)),
            dma((5,)), dma((5,)), dma((4,)), dma((nc,))],
        compiler_params=pltpu.CompilerParams(collective_id=collective_id, has_side_effects=True,
                                             vmem_limit_bytes=60 * 1024 * 1024),
    )(x_rows, og_rows, pre, scaled, both, prob, hot_expert, hot_token, probs, base, extra, tokens)


def local(tokens, out_grad, saved_pre, router_weight, slot_expert, slot_of, slot_weight):
    ne = lax.axis_size("expert")
    nd = lax.axis_size("dp")
    rows, width = tokens.shape
    top = slot_of.shape[1]
    half = saved_pre.shape[2] // 2
    experts = router_weight.shape[1]
    slots = slot_expert.shape[0]
    per = rows * top // ne
    total = rows * top

    group = slot_of // nd
    named = group[:, :, None] == jnp.arange(ne, dtype=jnp.int32)[None, None, :]
    names = jnp.sum(named.astype(F32), axis=1)
    before = (lax.broadcasted_iota(jnp.int32, (rows, rows), 1) < lax.broadcasted_iota(jnp.int32, (rows, rows), 0))
    arrival = jnp.dot(before.astype(BF), names.astype(BF), preferred_element_type=F32)
    rank = jnp.sum(jnp.where(named, arrival[:, None, :], 0.0), axis=2).astype(jnp.int32)
    place = (group * per + rank).reshape(-1)
    perm = place[None, :] == lax.broadcasted_iota(jnp.int32, (total, total), 0)
    perm = perm.astype(BF)
    pick = jnp.sum(perm.reshape(total, rows, top).astype(F32), axis=2).astype(BF)

    slot_hot = slot_of[:, :, None] == jnp.arange(slots, dtype=jnp.int32)[None, None, :]
    expert_ids = jnp.sum(jnp.where(slot_hot, slot_expert[None, None, :], 0), axis=2)
    first_expert = jnp.repeat(slot_expert.reshape(ne, nd)[:, 0], nd)
    is_low = jnp.sum(jnp.where(slot_hot, (slot_expert == first_expert).astype(jnp.int32)[None, None, :], 0), axis=2)

    wide_tokens = tokens.astype(F32)
    logits = jnp.dot(wide_tokens, router_weight, precision=lax.Precision.HIGHEST)
    log_total = jax.nn.logsumexp(logits, axis=1)
    router_probs = jnp.exp(logits - log_total[:, None])
    chosen = expert_ids[:, :, None] == jnp.arange(experts, dtype=jnp.int32)[None, None, :]
    chosen_prob = jnp.sum(jnp.where(chosen, router_probs[:, None, :], 0.0), axis=2).astype(BF)
    counts = jnp.sum(chosen.astype(jnp.int32), axis=(0, 1))

    hot = pick.reshape(2, ne // 4, 2, per, rows).transpose(1, 0, 2, 3, 4).reshape(ne // 4, 4 * per, rows)
    sv_send = jnp.dot(perm, saved_pre.reshape(total, 2 * half), preferred_element_type=F32).astype(BF)
    sv_send = sv_send.reshape(ne, per, 2 * half)
    facts = jnp.stack([chosen_prob.reshape(-1), is_low.reshape(-1).astype(BF)], axis=1)
    facts = jnp.dot(perm, facts, preferred_element_type=F32).astype(BF).reshape(ne, per, 2)
    facts = jnp.transpose(facts, (0, 2, 1))
    facts = jnp.pad(facts, ((0, 0), (0, 14), (0, 128 - per)))

    og, x, sv, got, both = forward_exchange(tokens, out_grad, sv_send, facts, hot, slot_weight[0], ne, nd, 1)
    og, sv, x = og.reshape(total, width), sv.reshape(total, 2 * half), x.reshape(total, width)
    prob = got[:, 0, :per].reshape(total).astype(F32)[:, None]
    low = got[:, 1, :per].reshape(total)[:, None] > 0
    down = both[:, :, :, 2 * half:].reshape(2, width, half)

    gate = sv[:, :half].astype(F32)
    up = sv[:, half:].astype(F32)
    sig = jax.nn.sigmoid(gate)
    active = gate * sig
    hidden = active * up
    back = jnp.where(low, jnp.dot(og, down[0], preferred_element_type=F32),
                     jnp.dot(og, down[1], preferred_element_type=F32))
    prob_grad = jnp.sum(back * hidden, axis=1).astype(BF)
    prob_send = jnp.broadcast_to(prob_grad[:, None], (total, 128)).reshape(ne, per, 128)

    scaled = (prob * hidden).astype(BF)
    hg = prob * back
    pre = jnp.concatenate([hg * up * sig * (1.0 + gate * (1.0 - sig)), hg * active], axis=1).astype(BF)
    zero = jnp.zeros((), BF)
    pre_both = jnp.concatenate([jnp.where(low, pre, zero), jnp.where(low, zero, pre)], axis=1)
    scaled_both = jnp.concatenate([jnp.where(low, scaled, zero), jnp.where(low, zero, scaled)], axis=1)

    hot_expert = jnp.dot(perm, chosen.reshape(total, experts).astype(BF), preferred_element_type=F32).astype(BF)
    wide = ((0, 0), (0, 128 - experts))
    base = (balance_coef * experts * counts.astype(F32) / total)[None, :]
    extra = 2.0 * zloss_coef * log_total[:, None] * router_probs
    part_back, sums, router_all, logits_grad = backward_exchange(
        x, og, pre_both, scaled_both, both, prob_send, jnp.pad(hot_expert, wide), pick.T, jnp.pad(router_probs, wide),
        jnp.pad(base, wide), jnp.pad(extra, wide), tokens, ne, nd, 3)
    logits_grad = logits_grad[:, :experts]
    expert_part = lax.dot_general(pick, part_back.reshape(total, width), (((0,), (0,)), ((), ())),
                                  preferred_element_type=F32)
    router_part = jnp.dot(logits_grad, router_weight.T, precision=lax.Precision.HIGHEST)
    token_grad = (expert_part + router_part).astype(BF)
    router_grad = jnp.transpose(router_all, (0, 2, 1, 3)).reshape(experts, width).T

    low_grad = jnp.concatenate([sums[1], sums[0, :, :half]], axis=1)
    high_grad = jnp.concatenate([sums[2], sums[0, :, half:]], axis=1)
    e = lax.axis_index("expert")
    low_first = slot_expert[e * nd] == 2 * e
    expert_grads = jnp.stack([jnp.where(low_first, low_grad, high_grad),
                              jnp.where(low_first, high_grad, low_grad)], axis=1)
    return (token_grad, expert_grads, router_grad)


def solution(mesh):
    placed = (
        P(("expert", "dp"), None),
        P(("expert", "dp"), None),
        P(("expert", "dp"), None, None),
        P(),
        P(),
        P(("expert", "dp"), None),
        P(("expert", "dp"), None, None),
    )
    return jax.shard_map(
        local,
        mesh=mesh,
        in_specs=placed,
        out_specs=(P(("expert", "dp"), None), P("dp", "expert", None), P()),
        check_vma=False,
    )
```

time: 614 us -> 462 us (0.75); the launches traced: 602 us -> 459 us
  Pallas kernels: 497 us -> 404 us
  matrix products: 73.4 us -> 15.3 us
    pallas_call x3 -> x2, Pallas kernels: 497 us -> 404 us  [the longest x1 208 us: backward_exchange(): pl.pallas_call(kernel, out_shape=[shape((ne, per, width), BF), shape((nc,...]
    dot_general x10 -> x3, matrix products: 62.8 us -> 7.44 us  [the longest x1 4.12 us: local(): jnp.dot(og, down[1], preferred_element_type=F32)]
where the time goes in v2:
time: 462 us; the launch traced here: 459 us
  Pallas kernels  404 us (87%)
  local copies, waits for them, and re-layouts  21.7 us (5%)
  other arithmetic  16.1 us (3%)
  matrix products  15.3 us (3%)
    pallas_call x1, Pallas kernels, backward_exchange(): pl.pallas_call(kernel, out_shape=[shape((ne, per, width), BF), shape((nc,...  208 us
    pallas_call x1, Pallas kernels, forward_exchange(): pl.pallas_call(kernel, out_shape=[shape((ne, per, width), BF), shape((ne,...  196 us
    unnamed x29, local copies, waits for them, and re-layouts  9.37 us

profile of v2, /device:TPU:2, one launch (start us, length us, event | category | flops | bytes accessed | tf_op | source)
XLA Modules:
  0.0 458.6 jit_solution(258316266024445314)
XLA Ops:
  0.6 0.0 copy-start
  0.7 2.0 fusion.33
  2.7 0.1 copy.62
  2.8 0.1 broadcast_multiply_fusion
  3.0 0.1 copy.64
  3.0 0.8 copy.60
  3.8 0.8 reshape.264
  4.6 0.1 slice_reduce_fusion
  4.7 0.1 broadcast_in_dim.122
  4.8 0.1 reshape.265
  4.9 0.7 compare_convert_fusion
  5.6 5.3 %select_reduce_fusion.1 = (s32[128,8]{1,0:T(8,128)S(1)}, s32[128,8]{1,0:T(8,128)S(1)}) fusion(s32[256]{0:T(256)} %param.11, s32[128,8]{1,0:T(8,128)S(1)} %copy.60, s32[256]{0:T(256)S(1)} %compare_convert_fusion), kind=kLoop, calls=%fused_computation.39 | loop fusion | flops 1308672 | bytes 14336 | tf_op jit(solution)/shard_map/reduce_sum | solution.py:578
  10.9 0.1 select_reduce_fusion.2
  11.0 0.1 copy.65
  11.1 0.1 convert_element_type.118
  11.2 0.7 add_select_fusion
  11.9 0.1 fusion.24
  12.1 0.1 copy.59
  12.2 0.1 eq.74
  12.3 0.1 convert_element_type.121
  12.5 0.8 fusion.21
  13.2 0.1 reshape.266
  13.4 0.0 copy-start.2
  13.4 0.0 copy-start.6
  13.4 2.3 fusion.17
  15.8 1.9 fusion.12
  17.8 195.8 %shard_map.94 = (bf16[32,32,2048]{2,1,0:T(8,128)(2,1)S(1)}, bf16[32,32,2048]{2,1,0:T(8,128)(2,1)S(1)}, bf16[32,32,1024]{2,1,0:T(8,128)(2,1)S(1)}, bf16[32,16,128...) custom-call(bf16[128,2048]{1,0:T(8,128)(2,1)S(1)} %copy-done.2, bf16[128,2048]{1,0:T(8,128)(2,1)S(1)} %copy-done.6, ...), custom_call_target="tpu_custom_call" | custom-call | tf_op jit(solution)/shard_map/pallas_call | solution.py:260
  213.6 1.9 copy-done.3
  215.5 2.0 copy-done.5
  217.4 0.1 compare_reduce_fusion
  217.5 0.1 gt.16
  217.6 0.1 reshape.274
  217.7 1.2 broadcast_select_fusion.3
  218.9 0.2 broadcast_select_fusion.2
  219.1 1.6 pad_maximum_fusion.2.sc
  220.8 2.7 fusion.32
  223.4 0.8 copy-done.4
  224.2 2.3 fusion.34
  226.6 4.1 fusion.7
  230.7 1.1 broadcast_select_fusion.1
  231.8 2.4 pad_maximum_fusion.pr
  234.2 0.1 convert_element_type.129
  234.3 0.9 broadcast_in_dim.128.qr
  235.2 0.6 pad.21.pb
  235.8 0.6 pad.23.ex
  236.4 0.1 eq.84
  236.5 1.0 fusion.20
  237.5 0.2 copy.70
  237.7 0.8 pad.20.he
  238.5 0.8 copy.71
  239.3 0.1 convert_reduce_fusion
  239.4 0.5 pad.22.ba
  240.0 208.2 %shard_map.95 = (bf16[32,32,2048]{2,1,0:T(8,128)(2,1)}, bf16[3,256,1024]{2,1,0:T(8,128)(2,1)}, f32[8,16,8,128]{3,2,1,0:T(8,128)}, f32[128,128]{1,0:T(8,128)}) custom-call(bf16[1024,2048]{1,0:T(8,128)(2,1)} %bitcast.52, bf16[1024,2048]{1,0:T(8,128)(2,1)} %bitcast.49, bf16[1024,2048]{1,0:T(8,128)(2,1)} %pad_maximum_fusion.pr, ...), custom_call_target="tpu_custom_call" | custom-call | tf_op jit(solution)/shard_map/pallas_call | solution.py:533
  448.2 0.0 copy-start.12
  448.2 1.3 slice_bitcast_fusion.1
  449.4 1.1 slice_bitcast_fusion.3
  450.5 0.6 dynamic_slice.3
  451.8 0.3 broadcast_select_fusion.5
  452.1 0.1 pad_maximum_fusion.3
  452.2 2.8 copy.72
  455.0 0.7 fusion.35
  455.8 0.3 copy-done.8
  456.0 1.8 fusion.4
  457.8 0.8 copy.79
  (31 shorter events, 0.3 us)
Async XLA Ops:
  0.6 12.8 %copy-start = (bf16[128,8,1024]{2,1,0:T(8,128)(2,1)S(1)}, bf16[128,8,1024]{2,1,0:T(8,128)(2,1)}, u32[]{:S(2)}) copy-start(bf16[128,8,1024]{2,1,0:T(8,128)(2,1)} %param.9) | copy-start | bytes 6291460
  0.6 11.5 %copy-start.11 = (s32[128,8]{0,1:T(8,128)S(1)}, s32[128,8]{0,1:T(8,128)}, u32[]{:S(2)}) copy-start(s32[128,8]{0,1:T(8,128)} %param.12) | copy-start | bytes 12292
  13.4 4.3 copy-start.2
  13.4 4.3 copy-start.6
  213.5 1.9 copy-start.3
  215.5 2.0 copy-start.5
  220.7 3.5 copy-start.4
  448.2 2.4 copy-start.12
  452.1 2.9 copy-start.7
  455.0 1.0 copy-start.8
  455.0 1.0 copy-start.10
  455.0 3.6 copy-start.1
  455.8 2.1 copy-start.9

commit v3 on v2

v3 whole, which is shorter than its diff:
```python
import jax
import jax.numpy as jnp
from jax import lax
from jax.experimental import pallas as pl
from jax.experimental.pallas import tpu as pltpu
from jax.sharding import PartitionSpec as P

zloss_coef = 0.001
balance_coef = 0.01
MESH = pl.DeviceIdType.MESH
ANY = pl.BlockSpec(memory_space=pl.ANY)
BF = jnp.bfloat16
F32 = jnp.float32


def greet(ne, nd, with_expert, with_dp):
    e, d = lax.axis_index("expert"), lax.axis_index("dp")
    barrier = pltpu.get_barrier_semaphore()
    total = 0
    if with_expert:
        def one(i, _):
            pl.semaphore_signal(barrier, inc=1, device_id=(lax.rem(e + i, ne), d), device_id_type=MESH)
            return 0
        lax.fori_loop(1, ne, one, 0)
        total += ne - 1
    if with_dp:
        def two(i, _):
            pl.semaphore_signal(barrier, inc=1, device_id=(e, lax.rem(d + i, nd)), device_id_type=MESH)
            return 0
        lax.fori_loop(1, nd, two, 0)
        total += nd - 1
    pl.semaphore_wait(barrier, total)


def send_all(ne, srcs, dsts, send_sem, recv_sem, local_sem, first=1, last=None):
    e, d = lax.axis_index("expert"), lax.axis_index("dp")
    for n, (src, dst) in enumerate(zip(srcs, dsts)):
        def one(i, _):
            half = (i + 1) // 2
            odd = lax.rem(i, 2)
            off = odd * half + (1 - odd) * (ne - half)
            peer = lax.rem(e + off, ne)
            pltpu.make_async_remote_copy(
                src_ref=src.at[peer], dst_ref=dst.at[e],
                send_sem=send_sem.at[n], recv_sem=recv_sem.at[n],
                device_id=(peer, d), device_id_type=MESH).start()
            return 0
        lax.fori_loop(first, ne if last is None else last, one, 0)
        if first == 1:
            pltpu.make_async_copy(src.at[e], dst.at[e], local_sem.at[n]).start()


def wait_all(ne, srcs, dsts, send_sem, recv_sem, local_sem):
    e, d = lax.axis_index("expert"), lax.axis_index("dp")
    for n, (src, dst) in enumerate(zip(srcs, dsts)):
        pltpu.make_async_remote_copy(
            src_ref=src.at[pl.ds(0, ne - 1)], dst_ref=dst.at[pl.ds(0, ne - 1)],
            send_sem=send_sem.at[n], recv_sem=recv_sem.at[n],
            device_id=(lax.rem(e + 1, ne), d), device_id_type=MESH).wait()
        pltpu.make_async_copy(src.at[e], dst.at[e], local_sem.at[n]).wait()


def fused(tokens, out_grad, saved, facts, pick, weight, hot_expert, hot_token, probs, base, extra, ne, nd):
    rows, width = tokens.shape
    nz = pick.shape[0]
    nq = ne // nz
    per = saved.shape[1]
    half = saved.shape[2] // 2
    total = ne * per
    cols = weight.shape[1]
    wr = width // nd
    nc = 3
    cw = cols // nc
    gw = 2 * cw
    tile = 512
    hops = nz // 2
    nx = nd // 2
    two = width // nx
    one = width // nd
    experts = 2 * ne
    rp = experts // nd
    nchip = ne // 2
    rl = width // nchip
    st = 32
    slots = 4

    def kernel(tok, og, sv, fa, pk, w, he, ht, pb, ba, ex, both, back, ow, orouter, olg,
               ring, picked, hot, ov, xv, svv, fav, wv, pv, cv, qs, qv, hev, htv, pbv, bav, exv, tkv, lg,
               far, near, got_half, got_full, yout, yin,
               rpart, rbuf, racc, rcore, rmine, rpiece, rfull,
               in_sem, pk_sem, ring_send, ring_recv, sel_send, sel_recv, sel_local,
               send_sem, recv_sem, local_sem, root_send, piece_sem, y_send, y_recv,
               x_send, x_recv, r_send, r_recv,
               q_sem, q_local, p_send, p_recv, p_local, a_send, a_recv, b_send, b_recv, s_send, s_recv,
               t_send, t_recv, misc, fin_sem):
        e, d = lax.axis_index("expert"), lax.axis_index("dp")
        core = lax.rem(e, 2)
        z = lax.rem(e // 2, nz)
        hi = e // (2 * nz)
        quarter = hi * 2 + core

        def at(zz):
            return hi * (2 * nz) + zz * 2 + core

        loads = [pltpu.make_async_copy(og, ring.at[0, z], in_sem.at[0]),
                 pltpu.make_async_copy(tok, ring.at[1, z], in_sem.at[1]),
                 pltpu.make_async_copy(pk.at[z], hot.at[z], in_sem.at[2])]
        facts_in = [pltpu.make_async_copy(s, t, in_sem.at[3 + n]) for n, (s, t) in enumerate(
            ((he, hev), (ht, htv), (pb, pbv), (ba, bav), (ex, exv), (tok, tkv)))]
        for c in loads + facts_in:
            c.start()
        greet(ne, nd, True, True)

        order = (2, 0, 1)
        for side, root in ((0, 0), (1, nd - 1)):
            @pl.when(d == root)
            def _():
                for c in order:
                    span = pl.ds(c * cw, cw)
                    mine = (root // 2) * 2
                    pltpu.make_async_copy(
                        w.at[pl.ds(mine * wr, 2 * wr), span], both.at[side, root // 2, :, span],
                        piece_sem.at[side, c]).start()
                    for j in (1, 3, 2):
                        q = (root // 2 + j) % (nd // 2)
                        pltpu.make_async_remote_copy(
                            src_ref=w.at[pl.ds(q * 2 * wr, 2 * wr), span], dst_ref=both.at[side, q, :, span],
                            send_sem=root_send.at[side], recv_sem=piece_sem.at[side, c],
                            device_id=(e, q * 2 + root % 2), device_id_type=MESH).start()

        def hot_send(i, _):
            q = lax.rem(z + i, nz)
            pltpu.make_async_remote_copy(
                src_ref=pk.at[q], dst_ref=hot.at[z], send_sem=pk_sem.at[0], recv_sem=pk_sem.at[1],
                device_id=(at(q), d), device_id_type=MESH).start()
            return 0
        lax.fori_loop(1, nz, hot_send, 0)

        def ring_copy(n, direction, step):
            sign = 1 - 2 * direction
            block = lax.rem(z - sign * step + nz, nz)
            to = lax.rem(z + sign + nz, nz)
            part = pl.ds(0, rows) if step < hops - 1 else pl.ds(direction * (rows // 2), rows // 2)
            return pltpu.make_async_remote_copy(
                src_ref=ring.at[n, block, part], dst_ref=ring.at[n, block, part],
                send_sem=ring_send.at[n, direction, step], recv_sem=ring_recv.at[n, direction, step],
                device_id=(at(to), d), device_id_type=MESH)

        copies = {(n, g, s): ring_copy(n, g, s) for n in range(2) for g in range(2) for s in range(hops)}

        def rows_out(first, last):
            send_all(ne, [sv, fa], [svv, fav], send_sem, recv_sem, local_sem, first, last)

        def hot_wait():
            loads[2].wait()
            pltpu.make_async_remote_copy(
                src_ref=pk.at[pl.ds(0, nz - 1)], dst_ref=hot.at[pl.ds(0, nz - 1)],
                send_sem=pk_sem.at[0], recv_sem=pk_sem.at[1], device_id=(at(lax.rem(z + 1, nz)), d),
                device_id_type=MESH).wait()

        outs = (ov, xv)
        uses = [0, 0]

        def drain(n, slot):
            some = pl.ds(0, (nq - 1) * per)
            pltpu.make_async_remote_copy(
                src_ref=picked.at[n, slot, some], dst_ref=picked.at[n, slot, some],
                send_sem=sel_send.at[n, slot], recv_sem=sel_recv.at[n], device_id=(at(lax.rem(z + 1, nz)), d),
                device_id_type=MESH).wait_send()
            pltpu.make_async_copy(picked.at[n, slot, pl.ds(0, per)], outs[n].at[0], sel_local.at[n, slot]).wait()

        def choose(n, block):
            slot = uses[n] % slots
            if uses[n] >= slots:
                drain(n, slot)
            uses[n] += 1

            def pick_tile(i, _):
                span = pl.ds(pl.multiple_of(i * tile, tile), tile)
                picked[n, slot, :, span] = jnp.dot(
                    hot[block], ring[n, block, :, span], preferred_element_type=F32).astype(BF)
                return 0
            lax.fori_loop(0, width // tile, pick_tile, 0)
            src_index = at(block)

            def hand(i, _):
                q = lax.rem(quarter + i, nq)
                pltpu.make_async_remote_copy(
                    src_ref=picked.at[n, slot, pl.ds(pl.multiple_of(q * per, per), per)],
                    dst_ref=outs[n].at[src_index], send_sem=sel_send.at[n, slot], recv_sem=sel_recv.at[n],
                    device_id=((q // 2) * (2 * nz) + z * 2 + lax.rem(q, 2), d), device_id_type=MESH).start()
                return 0
            lax.fori_loop(1, nq, hand, 0)
            pltpu.make_async_copy(
                picked.at[n, slot, pl.ds(pl.multiple_of(quarter * per, per), per)],
                outs[n].at[src_index], sel_local.at[n, slot]).start()

        def rows_in(n):
            for slot in range(slots):
                drain(n, slot)
            far_rows = nz * (nq - 1)
            pltpu.make_async_remote_copy(
                src_ref=outs[n].at[pl.ds(0, far_rows)], dst_ref=outs[n].at[pl.ds(0, far_rows)],
                send_sem=sel_send.at[n, 0], recv_sem=sel_recv.at[n], device_id=(at(lax.rem(z + 1, nz)), d),
                device_id_type=MESH).wait_recv()

        pair = d + 1 - 2 * lax.rem(d, 2)
        x, y = d // 2, lax.rem(d, 2)
        nx = nd // 2

        def scattered(c):
            span = pl.ds(c * cw, cw)
            for side in range(2):
                @pl.when(y == side)
                def _():
                    pltpu.make_async_copy(
                        w.at[pl.ds(0, 2 * wr), span], both.at[side, x, :, span], piece_sem.at[side, c]).wait()

        def along_y(c):
            part = both.at[y, x, :, pl.ds(c * cw, cw)]
            return pltpu.make_async_remote_copy(
                src_ref=part, dst_ref=part, send_sem=y_send.at[c], recv_sem=y_recv.at[c],
                device_id=(e, pair), device_id_type=MESH)

        def along_x(c, g):
            part = both.at[pl.ds(0, 2), x, :, pl.ds(c * cw, cw)]
            to = lax.rem(x + 1 + 2 * g, nx)
            return pltpu.make_async_remote_copy(
                src_ref=part, dst_ref=part, send_sem=x_send.at[c, g], recv_sem=x_recv.at[c, g],
                device_id=(e, to * 2 + y), device_id_type=MESH)

        def relay(c, g):
            source = lax.rem(x + 3 - 2 * g, nx)
            part = both.at[g, source, :, pl.ds(c * cw, cw)]
            to = lax.rem(x + 1 + 2 * g, nx)
            return pltpu.make_async_remote_copy(
                src_ref=part, dst_ref=part, send_sem=r_send.at[c, g], recv_sem=r_recv.at[c, g],
                device_id=(e, to * 2 + y), device_id_type=MESH)

        ys = {c: along_y(c) for c in order}
        xs = {(c, g): along_x(c, g) for c in order for g in range(2)}
        rs = {(c, g): relay(c, g) for c in order for g in range(2)}

        def stage_y(c):
            scattered(c)
            ys[c].start()

        def stage_x(c):
            ys[c].wait()
            for g in range(2):
                xs[c, g].start()

        def stage_r(c):
            for g in range(2):
                xs[c, g].wait()
                rs[c, g].start()

        def portion(n):
            rows_out(max(1, n * ne // 4), (n + 1) * ne // 4)

        def ring_start(n):
            loads[n].wait()
            for g in range(2):
                copies[n, g, 0].start()

        def ring_step(n, s):
            for g in range(2):
                copies[n, g, s].wait()
                if s + 1 < hops:
                    copies[n, g, s + 1].start()
            if n == 0 and s < 3:
                portion(s + 1)
            choose(n, lax.rem(z + nz - s - 1, nz))
            if s + 1 < hops:
                choose(n, lax.rem(z + s + 1, nz))

        def relayed(c):
            for g in range(2):
                rs[c, g].wait()

        def down_in():
            relayed(2)
            c = pltpu.make_async_copy(both.at[pl.ds(0, 2), pl.ds(0, nx), :, pl.ds(2 * cw, cw)],
                                      wv.at[pl.ds(0, 2), pl.ds(0, nx), :, pl.ds(0, cw)], misc.at[1])
            c.start()
            c.wait()

        gate_in = pltpu.make_async_copy(both.at[pl.ds(0, 2), pl.ds(0, nx), :, pl.ds(0, gw)], wv, misc.at[2])

        def experts_back():
            wait_all(ne, [sv, fa], [svv, fav], send_sem, recv_sem, local_sem)
            nb = ne // 4

            def block(r, _):
                src = pl.ds(r * nb, nb)
                m = nb * per
                both_back = []
                for side in range(2):
                    value = jnp.zeros((m, half), F32)
                    for j in range(nx):
                        value = value + jnp.dot(ov[src, :, j * two:(j + 1) * two].reshape(m, two),
                                                wv[side, j, :, :half], preferred_element_type=F32)
                    both_back.append(value)
                info = fav[src].reshape(m, 128).astype(F32)
                prob, low = info[:, 0:1], info[:, 1:2]
                gradient = jnp.where(low > 0.5, both_back[0], both_back[1])
                saved_rows = svv[src].reshape(m, 2 * half).astype(F32)
                gate, up = saved_rows[:, :half], saved_rows[:, half:]
                sig = 1.0 / (1.0 + jnp.exp(-gate))
                active = gate * sig
                hidden = active * up
                q = jnp.sum(gradient * hidden, axis=1, keepdims=True)
                qs[src] = jnp.broadcast_to(q, (m, 128)).astype(BF).reshape(nb, per, 128)
                scaled = prob * hidden
                grad = prob * gradient
                gate_grad = grad * up * sig * (1.0 + gate * (1.0 - sig))
                up_grad = grad * active
                at_rows = pl.ds(pl.multiple_of(r * m, m), m)
                is_low = low > 0.5
                cv[at_rows, :half] = jnp.where(is_low, scaled, 0.0).astype(BF)
                cv[at_rows, half:] = jnp.where(is_low, 0.0, scaled).astype(BF)
                pv[at_rows, :half] = jnp.where(is_low, gate_grad, 0.0).astype(BF)
                pv[at_rows, half:2 * half] = jnp.where(is_low, up_grad, 0.0).astype(BF)
                pv[at_rows, 2 * half:3 * half] = jnp.where(is_low, 0.0, gate_grad).astype(BF)
                pv[at_rows, 3 * half:] = jnp.where(is_low, 0.0, up_grad).astype(BF)
                return 0
            lax.fori_loop(0, 4, block, 0)
            send_all(ne, [qs], [qv], q_sem.at[pl.ds(0, 1)], q_sem.at[pl.ds(1, 1)], q_local)

        plus, minus, across = lax.rem(x + 1, nx), lax.rem(x + 3, nx), lax.rem(x + 2, nx)

        def product(c, from_row, n):
            left, right, first_col = (ov, cv, 0) if c == 0 else (xv, pv, (c - 1) * gw)
            return lax.dot_general(
                left[:, :, pl.ds(from_row, n)].reshape(total, n), right[:, pl.ds(first_col, gw)],
                (((0,), (0,)), ((), ())), preferred_element_type=F32)

        def contribute(c, target, out):
            def piece(i, _):
                out[pl.ds(pl.multiple_of(i * one, one), one), :] = product(
                    c, pl.multiple_of(target * two + i * one, one), one).astype(BF)
                return 0
            lax.fori_loop(0, 2, piece, 0)

        def first(c, g):
            return pltpu.make_async_remote_copy(
                src_ref=far.at[c, pl.ds(g * one, one)], dst_ref=got_half.at[c, g],
                send_sem=a_send.at[c, g], recv_sem=a_recv.at[c, g],
                device_id=(e, (plus if g == 0 else minus) * 2 + y), device_id_type=MESH)

        def second(c, g):
            return pltpu.make_async_remote_copy(
                src_ref=near.at[c, g], dst_ref=got_full.at[c, g],
                send_sem=b_send.at[c, g], recv_sem=b_recv.at[c, g],
                device_id=(e, (plus if g == 0 else minus) * 2 + y), device_id_type=MESH)

        def swap(c):
            return pltpu.make_async_remote_copy(
                src_ref=yout.at[c], dst_ref=yin.at[c], send_sem=s_send.at[c], recv_sem=s_recv.at[c],
                device_id=(e, d + 1 - 2 * y), device_id_type=MESH)

        firsts = {(c, g): first(c, g) for c in range(nc) for g in range(2)}
        seconds = {(c, g): second(c, g) for c in range(nc) for g in range(2)}
        swaps = [swap(c) for c in range(nc)]

        def start_near(c):
            for g in range(2):
                firsts[c, g].wait()

                def add(i, _):
                    src = pl.ds(pl.multiple_of(i * st, st), st)
                    dst = pl.ds(pl.multiple_of(g * one + i * st, st), st)
                    near[c, g, dst, :] = (near[c, g, dst, :].astype(F32)
                                          + got_half[c, g, src, :].astype(F32)).astype(BF)
                    return 0
                lax.fori_loop(0, one // st, add, 0)
                seconds[c, g].start()

        def summed(c, side, finish):
            def add(i, _):
                src = pl.ds(pl.multiple_of(side * one + i * 128, 128), 128)
                into = pl.ds(pl.multiple_of(i * 128, 128), 128)
                value = product(c, pl.multiple_of(x * two + side * one + i * 128, 128), 128)
                value = value + got_full[c, 0, src, :].astype(F32) + got_full[c, 1, src, :].astype(F32)
                if finish:
                    value = value + yin[c, into, :].astype(F32)
                yout[c, into, :] = value.astype(BF)
                return 0
            lax.fori_loop(0, one // 128, add, 0)

        def start_swap(c):
            for g in range(2):
                seconds[c, g].wait()
            summed(c, 1 - y, False)
            swaps[c].start()

        def finish(c):
            swaps[c].wait()
            summed(c, y, True)
            pltpu.make_async_copy(yout.at[c], ow.at[c], fin_sem.at[c]).start()

        def start_far(c):
            contribute(c, across, far.at[c])
            for g in range(2):
                firsts[c, g].start()

        def near_both(c):
            contribute(c, plus, near.at[c, 0])
            contribute(c, minus, near.at[c, 1])

        def part_tile(j, _):
            contract = (((1,), (1,)), ((), ()))
            w_rows = pl.ds(pl.multiple_of(lax.rem(j, 2) * one, one), one)
            value = lax.dot_general(pv[:, :gw], wv[0, j // 2, w_rows, :], contract, preferred_element_type=F32)
            value = value + lax.dot_general(pv[:, gw:], wv[1, j // 2, w_rows, :], contract, preferred_element_type=F32)
            ring[0, :, :, pl.ds(pl.multiple_of(j * one, one), one)] = value.astype(BF).reshape(nz, rows, one)
            return 0

        def part_send(i, _):
            half_i = (i + 1) // 2
            odd = lax.rem(i, 2)
            peer = lax.rem(e + odd * half_i + (1 - odd) * (ne - half_i), ne)
            pltpu.make_async_remote_copy(
                src_ref=ring.at[0, peer // nq, pl.ds(pl.multiple_of(lax.rem(peer, nq) * per, per), per)],
                dst_ref=back.at[e], send_sem=p_send.at[0], recv_sem=p_recv.at[0],
                device_id=(peer, d), device_id_type=MESH).start()
            return 0

        def part_all():
            gate_in.wait()
            lax.fori_loop(0, nd, part_tile, 0)
            lax.fori_loop(1, ne, part_send, 0)
            pltpu.make_async_copy(
                ring.at[0, e // nq, pl.ds(pl.multiple_of(lax.rem(e, nq) * per, per), per)], back.at[e],
                p_local.at[0]).start()

        ring_start(0)
        portion(0)
        hot_wait()
        choose(0, z)
        stage_y(order[0])
        stage_y(order[1])
        ring_step(0, 0)
        ring_start(1)
        stage_x(order[0])
        stage_y(order[2])
        choose(1, z)
        ring_step(0, 1)
        stage_x(order[1])
        stage_r(order[0])
        ring_step(0, 2)
        stage_x(order[2])
        ring_step(0, 3)
        ring_step(1, 0)
        stage_r(order[1])
        down_in()
        rows_in(0)
        experts_back()
        stage_r(order[2])
        ring_step(1, 1)
        start_far(0)
        ring_step(1, 2)
        near_both(0)
        ring_step(1, 3)
        start_near(0)
        for c in order[1:]:
            relayed(c)
        gate_in.start()
        rows_in(1)
        start_far(1)
        start_far(2)
        for c in facts_in:
            c.wait()
        wait_all(ne, [qs], [qv], q_sem.at[pl.ds(0, 1)], q_sem.at[pl.ds(1, 1)], q_local)
        chosen = hev[...] * qv[...].reshape(total, 128)
        grad = jnp.dot(htv[...], chosen, preferred_element_type=F32) + bav[...]
        inner = jnp.sum(pbv[...] * grad, axis=1, keepdims=True)
        grad = pbv[...] * (grad - inner) + exv[...]
        lg[...] = grad
        lg_out = pltpu.make_async_copy(lg, olg, misc.at[3])
        lg_out.start()
        turned = grad.T[:experts]
        high = turned.astype(BF)
        rest = turned - high.astype(F32)
        middle = rest.astype(BF)
        low = (rest - middle.astype(F32)).astype(BF)

        def router_tile(i, _):
            span = pl.ds(pl.multiple_of(i * 512, 512), 512)
            t = tkv[:, span]
            rpart[:, span] = (jnp.dot(low, t, preferred_element_type=F32)
                              + jnp.dot(middle, t, preferred_element_type=F32)
                              + jnp.dot(high, t, preferred_element_type=F32))
            return 0
        lax.fori_loop(0, width // 512, router_tile, 0)

        def rs_dp(i, _):
            q = lax.rem(d + i, nd)
            pltpu.make_async_remote_copy(
                src_ref=rpart.at[pl.ds(pl.multiple_of(q * rp, rp), rp)], dst_ref=rbuf.at[d],
                send_sem=t_send.at[0], recv_sem=t_recv.at[0], device_id=(e, q), device_id_type=MESH).start()
            return 0
        lax.fori_loop(1, nd, rs_dp, 0)
        rbuf[d] = rpart[pl.ds(pl.multiple_of(d * rp, rp), rp), :]

        near_both(1)
        start_near(1)
        pltpu.make_async_remote_copy(
            src_ref=rbuf.at[pl.ds(0, nd - 1)], dst_ref=rbuf.at[pl.ds(0, nd - 1)],
            send_sem=t_send.at[0], recv_sem=t_recv.at[0], device_id=(e, lax.rem(d + 1, nd)),
            device_id_type=MESH).wait()
        racc[...] = jnp.sum(rbuf[...], axis=0)
        mate = e + 1 - 2 * lax.rem(e, 2)
        core = lax.rem(e, 2)
        chip = e // 2
        cc = pltpu.make_async_remote_copy(
            src_ref=racc, dst_ref=rcore, send_sem=t_send.at[1], recv_sem=t_recv.at[1],
            device_id=(mate, d), device_id_type=MESH)
        cc.start()

        cc.wait()
        for n in range(nchip):
            rmine[n] = racc[:, n * rl:(n + 1) * rl] + rcore[:, n * rl:(n + 1) * rl]

        def rs_chip(i, _):
            q = lax.rem(chip + i, nchip)
            pltpu.make_async_remote_copy(
                src_ref=rmine.at[q], dst_ref=rpiece.at[chip], send_sem=t_send.at[2], recv_sem=t_recv.at[2],
                device_id=(q * 2 + core, d), device_id_type=MESH).start()
            return 0
        lax.fori_loop(1, nchip, rs_chip, 0)
        rpiece[chip] = rmine[chip]

        pltpu.make_async_remote_copy(
            src_ref=rpiece.at[pl.ds(0, nchip - 1)], dst_ref=rpiece.at[pl.ds(0, nchip - 1)],
            send_sem=t_send.at[2], recv_sem=t_recv.at[2], device_id=(mate, d), device_id_type=MESH).wait()
        rfull[chip] = jnp.sum(rpiece[...], axis=0)

        def ag_chip(i, _):
            q = lax.rem(chip + i, nchip)
            pltpu.make_async_remote_copy(
                src_ref=rfull.at[chip], dst_ref=rfull.at[chip], send_sem=t_send.at[3], recv_sem=t_recv.at[3],
                device_id=(q * 2 + core, d), device_id_type=MESH).start()
            return 0
        lax.fori_loop(1, nchip, ag_chip, 0)

        part_all()
        near_both(2)
        start_near(2)
        pltpu.make_async_remote_copy(
            src_ref=rfull.at[pl.ds(0, nchip - 1)], dst_ref=rfull.at[pl.ds(0, nchip - 1)],
            send_sem=t_send.at[3], recv_sem=t_recv.at[3], device_id=(mate, d), device_id_type=MESH).wait()

        def ag_dp(i, _):
            q = lax.rem(d + i, nd)
            pltpu.make_async_remote_copy(
                src_ref=rfull, dst_ref=orouter.at[d], send_sem=t_send.at[4], recv_sem=t_recv.at[4],
                device_id=(e, q), device_id_type=MESH).start()
            return 0
        lax.fori_loop(1, nd, ag_dp, 0)
        own_f = pltpu.make_async_copy(rfull, orouter.at[d], misc.at[0])
        own_f.start()

        start_swap(0)
        start_swap(1)
        finish(0)
        start_swap(2)
        finish(1)
        finish(2)

        pltpu.make_async_remote_copy(
            src_ref=orouter.at[pl.ds(0, nd - 1)], dst_ref=orouter.at[pl.ds(0, nd - 1)],
            send_sem=t_send.at[4], recv_sem=t_recv.at[4], device_id=(e, lax.rem(d + 1, nd)),
            device_id_type=MESH).wait()
        own_f.wait()
        lg_out.wait()
        pltpu.make_async_remote_copy(
            src_ref=back.at[pl.ds(0, ne - 1)], dst_ref=back.at[pl.ds(0, ne - 1)],
            send_sem=p_send.at[0], recv_sem=p_recv.at[0], device_id=(mate, d), device_id_type=MESH).wait()
        pltpu.make_async_copy(
            ring.at[0, e // nq, pl.ds(pl.multiple_of(lax.rem(e, nq) * per, per), per)], back.at[e],
            p_local.at[0]).wait()
        for c in range(nc):
            pltpu.make_async_copy(yout.at[c], ow.at[c], fin_sem.at[c]).wait()
        for side, root in ((0, 0), (1, nd - 1)):
            @pl.when(d == root)
            def _():
                pltpu.make_async_remote_copy(
                    src_ref=both.at[side, pl.ds(0, nx - 1)], dst_ref=both.at[side, pl.ds(0, nx - 1)],
                    send_sem=root_send.at[side], recv_sem=piece_sem.at[side, 0],
                    device_id=(e, (root + 2) % nd), device_id_type=MESH).wait_send()

    dma = pltpu.SemaphoreType.DMA
    shape = jax.ShapeDtypeStruct
    vmem = pltpu.VMEM
    return pl.pallas_call(
        kernel,
        out_shape=[shape((2, nx, two, cols), BF), shape((ne, per, width), BF), shape((nc, one, gw), BF),
                   shape((nd, nchip, rp, rl), F32), shape((rows, 128), F32)],
        in_specs=[ANY] * 11, out_specs=[ANY] * 5,
        scratch_shapes=[
            vmem((2, nz, rows, width), BF), vmem((2, slots, rows, width), BF), vmem((nz, nq * per, rows), BF),
            vmem((ne, per, width), BF), vmem((ne, per, width), BF), vmem(saved.shape, BF), vmem(facts.shape, BF),
            vmem((2, nx, two, gw), BF), vmem((total, 2 * gw), BF), vmem((total, gw), BF),
            vmem((ne, per, 128), BF), vmem((ne, per, 128), BF), vmem((total, 128), BF), vmem((rows, total), BF),
            vmem((rows, 128), F32), vmem((1, 128), F32), vmem((rows, 128), F32), vmem((rows, width), BF),
            vmem((rows, 128), F32),
            vmem((nc, two, gw), BF), vmem((nc, 2, two, gw), BF),
            vmem((nc, 2, one, gw), BF), vmem((nc, 2, two, gw), BF), vmem((nc, one, gw), BF), vmem((nc, one, gw), BF),
            vmem((experts, width), F32), vmem((nd, rp, width), F32), vmem((rp, width), F32), vmem((rp, width), F32),
            vmem((nchip, rp, rl), F32), vmem((nchip, rp, rl), F32), vmem((nchip, rp, rl), F32),
            dma((9,)), dma((2,)), dma((2, 2, hops)), dma((2, 2, hops)), dma((2, slots)), dma((2,)), dma((2, slots)),
            dma((2,)), dma((2,)), dma((2,)), dma((2,)), dma((2, nc)), dma((nc,)), dma((nc,)),
            dma((nc, 2)), dma((nc, 2)), dma((nc, 2)), dma((nc, 2)),
            dma((2,)), dma((1,)), dma((1,)), dma((1,)), dma((1,)), dma((nc, 2)), dma((nc, 2)), dma((nc, 2)),
            dma((nc, 2)), dma((nc,)), dma((nc,)),
            dma((5,)), dma((5,)), dma((4,)), dma((nc,))],
        compiler_params=pltpu.CompilerParams(collective_id=1, has_side_effects=True,
                                             vmem_limit_bytes=63 * 1024 * 1024),
    )(tokens, out_grad, saved, facts, pick, weight, hot_expert, hot_token, probs, base, extra)


def local(tokens, out_grad, saved_pre, router_weight, slot_expert, slot_of, slot_weight):
    ne = lax.axis_size("expert")
    nd = lax.axis_size("dp")
    rows, width = tokens.shape
    top = slot_of.shape[1]
    half = saved_pre.shape[2] // 2
    experts = router_weight.shape[1]
    slots = slot_expert.shape[0]
    per = rows * top // ne
    total = rows * top

    group = slot_of // nd
    named = group[:, :, None] == jnp.arange(ne, dtype=jnp.int32)[None, None, :]
    names = jnp.sum(named.astype(F32), axis=1)
    before = (lax.broadcasted_iota(jnp.int32, (rows, rows), 1) < lax.broadcasted_iota(jnp.int32, (rows, rows), 0))
    arrival = jnp.dot(before.astype(BF), names.astype(BF), preferred_element_type=F32)
    rank = jnp.sum(jnp.where(named, arrival[:, None, :], 0.0), axis=2).astype(jnp.int32)
    place = (group * per + rank).reshape(-1)
    perm = place[None, :] == lax.broadcasted_iota(jnp.int32, (total, total), 0)
    perm = perm.astype(BF)
    pick = jnp.sum(perm.reshape(total, rows, top).astype(F32), axis=2).astype(BF)

    slot_hot = slot_of[:, :, None] == jnp.arange(slots, dtype=jnp.int32)[None, None, :]
    expert_ids = jnp.sum(jnp.where(slot_hot, slot_expert[None, None, :], 0), axis=2)
    first_expert = jnp.repeat(slot_expert.reshape(ne, nd)[:, 0], nd)
    is_low = jnp.sum(jnp.where(slot_hot, (slot_expert == first_expert).astype(jnp.int32)[None, None, :], 0), axis=2)

    wide_tokens = tokens.astype(F32)
    logits = jnp.dot(wide_tokens, router_weight, precision=lax.Precision.HIGHEST)
    log_total = jax.nn.logsumexp(logits, axis=1)
    router_probs = jnp.exp(logits - log_total[:, None])
    chosen = expert_ids[:, :, None] == jnp.arange(experts, dtype=jnp.int32)[None, None, :]
    chosen_prob = jnp.sum(jnp.where(chosen, router_probs[:, None, :], 0.0), axis=2).astype(BF)
    counts = jnp.sum(chosen.astype(jnp.int32), axis=(0, 1))

    hot = pick.reshape(2, ne // 4, 2, per, rows).transpose(1, 0, 2, 3, 4).reshape(ne // 4, 4 * per, rows)
    sv_send = jnp.dot(perm, saved_pre.reshape(total, 2 * half), preferred_element_type=F32).astype(BF)
    sv_send = sv_send.reshape(ne, per, 2 * half)
    chosen_row = chosen.reshape(total, experts)
    facts = jnp.concatenate([chosen_prob.reshape(-1, 1), is_low.reshape(-1, 1).astype(BF)], axis=1)
    facts = jnp.pad(facts, ((0, 0), (0, 126)))
    facts = jnp.dot(perm, facts, preferred_element_type=F32).astype(BF).reshape(ne, per, 128)
    wide = ((0, 0), (0, 128 - experts))
    hot_expert = jnp.dot(perm, jnp.pad(chosen_row.astype(BF), wide), preferred_element_type=F32).astype(BF)
    base = (balance_coef * experts * counts.astype(F32) / total)[None, :]
    extra = 2.0 * zloss_coef * log_total[:, None] * router_probs

    _, part_back, sums, router_all, logits_grad = fused(
        tokens, out_grad, sv_send, facts, hot, slot_weight[0], hot_expert, pick.T, jnp.pad(router_probs, wide),
        jnp.pad(base, wide), jnp.pad(extra, wide), ne, nd)
    logits_grad = logits_grad[:, :experts]
    expert_part = lax.dot_general(pick, part_back.reshape(total, width), (((0,), (0,)), ((), ())),
                                  preferred_element_type=F32)
    router_part = jnp.dot(logits_grad, router_weight.T, precision=lax.Precision.HIGHEST)
    token_grad = (expert_part + router_part).astype(BF)
    router_grad = jnp.transpose(router_all, (0, 2, 1, 3)).reshape(experts, width).T

    low_grad = jnp.concatenate([sums[1], sums[0, :, :half]], axis=1)
    high_grad = jnp.concatenate([sums[2], sums[0, :, half:]], axis=1)
    e = lax.axis_index("expert")
    low_first = slot_expert[e * nd] == 2 * e
    expert_grads = jnp.stack([jnp.where(low_first, low_grad, high_grad),
                              jnp.where(low_first, high_grad, low_grad)], axis=1)
    return (token_grad, expert_grads, router_grad)


def solution(mesh):
    placed = (
        P(("expert", "dp"), None),
        P(("expert", "dp"), None),
        P(("expert", "dp"), None, None),
        P(),
        P(),
        P(("expert", "dp"), None),
        P(("expert", "dp"), None, None),
    )
    return jax.shard_map(
        local,
        mesh=mesh,
        in_specs=placed,
        out_specs=(P(("expert", "dp"), None), P("dp", "expert", None), P()),
        check_vma=False,
    )
```

time: 462 us -> 397 us (0.86)
  Pallas kernels: 404 us -> 357 us
  local copies, waits for them, and re-layouts: 21.7 us -> 13.6 us
  other arithmetic: 16.1 us -> 9.69 us
    pallas_call x2 -> x1, Pallas kernels: 404 us -> 357 us  [fused(): pl.pallas_call(kernel, out_shape=[shape((2, nx, two, cols), BF), shape((n...]
    dot_general x3 -> x1, matrix products: 7.44 us -> 1.54 us  [local(): jnp.dot(perm, jnp.pad(chosen_row.astype(BF), wide), preferred_element_typ...]
    unnamed x29 -> x17, local copies, waits for them, and re-layouts: 9.37 us -> 5.5 us
where the time goes in v3:
time: 397 us; the launch traced here: 392 us
  Pallas kernels  357 us (90%)
  local copies, waits for them, and re-layouts  13.6 us (3%)
  matrix products  11.1 us (3%)
  other arithmetic  9.69 us (2%)
    pallas_call x1, Pallas kernels, fused(): pl.pallas_call(kernel, out_shape=[shape((2, nx, two, cols), BF), shape((n...  357 us

profile of v3, /device:TPU:2, one launch (start us, length us, event | category | flops | bytes accessed | tf_op | source)
XLA Modules:
  0.0 392.5 jit_solution(9354946603717021663)
XLA Ops:
  0.6 0.0 copy-start
  0.6 0.0 copy-start.4
  0.7 1.0 copy-done
  1.7 1.7 fusion.34
  3.4 0.1 copy.47
  3.5 0.1 broadcast_multiply_fusion
  3.7 0.1 copy.49
  3.7 0.8 copy.45
  4.5 0.8 reshape.226
  5.3 0.1 slice_reduce_fusion
  5.4 0.1 broadcast_in_dim.69
  5.5 0.1 reshape.227
  5.6 0.7 compare_convert_fusion
  6.3 5.3 %select_reduce_fusion.1 = (s32[128,8]{1,0:T(8,128)S(1)}, s32[128,8]{1,0:T(8,128)S(1)}) fusion(s32[256]{0:T(256)} %param.11, s32[128,8]{1,0:T(8,128)S(1)} %copy.45, s32[256]{0:T(256)S(1)} %compare_convert_fusion), kind=kLoop, calls=%fused_computation.18 | loop fusion | flops 1308672 | bytes 14336 | tf_op jit(solution)/shard_map/reduce_sum | solution.py:646
  11.6 0.1 select_reduce_fusion.2
  11.7 0.1 copy.50
  11.8 0.1 convert_element_type.89
  11.9 0.7 add_select_fusion
  12.6 0.1 fusion.26
  12.8 0.0 copy-done.4
  12.8 0.1 copy.44
  12.9 0.1 eq.74
  13.1 0.1 convert_element_type.92
  13.2 0.0 copy-start.6
  13.2 1.5 fusion.13
  14.6 0.6 pad.25.pb
  15.3 0.6 pad.27.ex
  15.9 0.1 eq.84
  16.0 0.2 iota_compare_fusion.13
  16.2 1.5 fusion.14.he
  17.7 0.0 copy-done.6
  17.7 3.7 fusion.10
  21.4 1.9 fusion.5
  23.4 0.7 copy.51
  24.1 0.8 copy.52
  24.9 0.1 convert_reduce_fusion
  25.1 0.5 pad.26.ba
  25.6 356.6 %shard_map.94 = (bf16[2,4,512,1536]{3,2,1,0:T(8,128)(2,1)}, bf16[32,32,2048]{2,1,0:T(8,128)(2,1)}, bf16[3,256,1024]{2,1,0:T(8,128)(2,1)}, f32[8,16,8,128]{3,2,1,0:T(8,128)}, f32[128,128]{1,0:T(8,128)}) custom-call(bf16[128,2048]{1,0:T(8,128)(2,1)} %tok.1, bf16[128,2048]{1,0:T(8,128)(2,1)} %og.1, bf16[32,32,1024]{2,1,0:T(8,128)(2,1)} %bitcast.39, ...), custom_call_target="tpu_custom_call" | custom-call | tf_op jit(solution)/shard_map/pallas_call | solution.py:596
  382.2 0.0 copy-start.5
  382.2 1.3 slice_bitcast_fusion.1
  383.5 1.1 slice_bitcast_fusion.3
  384.5 0.0 copy-done.5
  384.6 0.6 dynamic_slice.3
  385.8 0.3 broadcast_select_fusion.1
  386.1 0.0 copy-start.1
  386.1 0.1 pad_maximum_fusion
  386.3 2.8 copy.53
  389.0 0.0 copy-done.1
  389.0 0.0 copy-start.3
  389.0 0.7 fusion.35
  389.8 0.0 copy-start.2
  389.8 0.1 copy-done.3
  389.9 1.8 fusion.4
  391.7 0.0 copy-done.2
  391.7 0.8 copy.58
  (9 shorter events, 0.2 us)
Async XLA Ops:
  0.6 1.0 copy-start
  0.6 12.2 %copy-start.4 = (s32[128,8]{0,1:T(8,128)S(1)}, s32[128,8]{0,1:T(8,128)}, u32[]{:S(2)}) copy-start(s32[128,8]{0,1:T(8,128)} %param.12) | copy-start | bytes 12292
  13.2 4.6 %copy-start.6 = (bf16[128,8,1024]{2,1,0:T(8,128)(2,1)S(1)}, bf16[128,8,1024]{2,1,0:T(8,128)(2,1)}, u32[]{:S(2)}) copy-start(bf16[128,8,1024]{2,1,0:T(8,128)(2,1)} %param.9) | copy-start | bytes 6291460
  382.2 2.4 copy-start.5
  386.1 2.9 copy-start.1
  389.0 0.8 copy-start.3
  389.8 1.9 copy-start.2

commit v4 on v3

--- a/solution.py
+++ b/solution.py
@@ -72,7 +72,7 @@
     nc = 3
     cw = cols // nc
     gw = 2 * cw
-    tile = 512
+    tile = 2048
     hops = nz // 2
     nx = nd // 2
     two = width // nx
@@ -268,8 +268,6 @@
                 copies[n, g, s].wait()
                 if s + 1 < hops:
                     copies[n, g, s + 1].start()
-            if n == 0 and s < 3:
-                portion(s + 1)
             choose(n, lax.rem(z + nz - s - 1, nz))
             if s + 1 < hops:
                 choose(n, lax.rem(z + s + 1, nz))
@@ -302,7 +300,7 @@
                                                 wv[side, j, :, :half], preferred_element_type=F32)
                     both_back.append(value)
                 info = fav[src].reshape(m, 128).astype(F32)
-                prob, low = info[:, 0:1], info[:, 1:2]
+                prob, low = info[:, experts:experts + 1], info[:, experts + 1:experts + 2]
                 gradient = jnp.where(low > 0.5, both_back[0], both_back[1])
                 saved_rows = svv[src].reshape(m, 2 * half).astype(F32)
                 gate, up = saved_rows[:, :half], saved_rows[:, half:]
@@ -436,39 +434,30 @@
 
         ring_start(0)
         portion(0)
+        portion(1)
         hot_wait()
+        portion(2)
         choose(0, z)
         stage_y(order[0])
+        ring_step(0, 0)
         stage_y(order[1])
-        ring_step(0, 0)
-        ring_start(1)
         stage_x(order[0])
         stage_y(order[2])
+        ring_step(0, 1)
+        ring_start(1)
+        stage_x(order[1])
+        ring_step(0, 2)
+        stage_r(order[0])
+        stage_x(order[2])
+        portion(3)
+        ring_step(0, 3)
         choose(1, z)
-        ring_step(0, 1)
-        stage_x(order[1])
-        stage_r(order[0])
-        ring_step(0, 2)
-        stage_x(order[2])
-        ring_step(0, 3)
+        stage_r(order[1])
         ring_step(1, 0)
-        stage_r(order[1])
         down_in()
         rows_in(0)
         experts_back()
-        stage_r(order[2])
-        ring_step(1, 1)
-        start_far(0)
-        ring_step(1, 2)
         near_both(0)
-        ring_step(1, 3)
-        start_near(0)
-        for c in order[1:]:
-            relayed(c)
-        gate_in.start()
-        rows_in(1)
-        start_far(1)
-        start_far(2)
         for c in facts_in:
             c.wait()
         wait_all(ne, [qs], [qv], q_sem.at[pl.ds(0, 1)], q_sem.at[pl.ds(1, 1)], q_local)
@@ -503,8 +492,8 @@
         lax.fori_loop(1, nd, rs_dp, 0)
         rbuf[d] = rpart[pl.ds(pl.multiple_of(d * rp, rp), rp), :]
 
-        near_both(1)
-        start_near(1)
+        start_far(0)
+        ring_step(1, 1)
         pltpu.make_async_remote_copy(
             src_ref=rbuf.at[pl.ds(0, nd - 1)], dst_ref=rbuf.at[pl.ds(0, nd - 1)],
             send_sem=t_send.at[0], recv_sem=t_recv.at[0], device_id=(e, lax.rem(d + 1, nd)),
@@ -518,6 +507,7 @@
             device_id=(mate, d), device_id_type=MESH)
         cc.start()
 
+        stage_r(order[2])
         cc.wait()
         for n in range(nchip):
             rmine[n] = racc[:, n * rl:(n + 1) * rl] + rcore[:, n * rl:(n + 1) * rl]
@@ -531,6 +521,8 @@
         lax.fori_loop(1, nchip, rs_chip, 0)
         rpiece[chip] = rmine[chip]
 
+        ring_step(1, 2)
+        start_near(0)
         pltpu.make_async_remote_copy(
             src_ref=rpiece.at[pl.ds(0, nchip - 1)], dst_ref=rpiece.at[pl.ds(0, nchip - 1)],
             send_sem=t_send.at[2], recv_sem=t_recv.at[2], device_id=(mate, d), device_id_type=MESH).wait()
@@ -544,8 +536,17 @@
             return 0
         lax.fori_loop(1, nchip, ag_chip, 0)
 
+        ring_step(1, 3)
+        for c in order[1:]:
+            relayed(c)
+        gate_in.start()
         part_all()
+        rows_in(1)
+        start_far(1)
+        near_both(1)
+        start_far(2)
         near_both(2)
+        start_near(1)
         start_near(2)
         pltpu.make_async_remote_copy(
             src_ref=rfull.at[pl.ds(0, nchip - 1)], dst_ref=rfull.at[pl.ds(0, nchip - 1)],
@@ -642,33 +643,31 @@
     perm = perm.astype(BF)
     pick = jnp.sum(perm.reshape(total, rows, top).astype(F32), axis=2).astype(BF)
 
-    slot_hot = slot_of[:, :, None] == jnp.arange(slots, dtype=jnp.int32)[None, None, :]
-    expert_ids = jnp.sum(jnp.where(slot_hot, slot_expert[None, None, :], 0), axis=2)
     first_expert = jnp.repeat(slot_expert.reshape(ne, nd)[:, 0], nd)
-    is_low = jnp.sum(jnp.where(slot_hot, (slot_expert == first_expert).astype(jnp.int32)[None, None, :], 0), axis=2)
+    lane = jnp.arange(128, dtype=jnp.int32)[None, :]
+    table = (lane == slot_expert[:, None]) | ((lane == experts + 1) & (slot_expert == first_expert)[:, None])
+    slot_hot = slot_of.reshape(-1, 1) == jnp.arange(slots, dtype=jnp.int32)[None, :]
+    info = jnp.dot(slot_hot.astype(BF), table.astype(BF), preferred_element_type=F32)
 
     wide_tokens = tokens.astype(F32)
     logits = jnp.dot(wide_tokens, router_weight, precision=lax.Precision.HIGHEST)
     log_total = jax.nn.logsumexp(logits, axis=1)
     router_probs = jnp.exp(logits - log_total[:, None])
-    chosen = expert_ids[:, :, None] == jnp.arange(experts, dtype=jnp.int32)[None, None, :]
-    chosen_prob = jnp.sum(jnp.where(chosen, router_probs[:, None, :], 0.0), axis=2).astype(BF)
-    counts = jnp.sum(chosen.astype(jnp.int32), axis=(0, 1))
+    wide = ((0, 0), (0, 128 - experts))
+    wide_probs = jnp.pad(router_probs, wide)
+    chosen_prob = jnp.sum(info.reshape(rows, top, 128) * wide_probs[:, None, :], axis=2)
+    counts = jnp.sum(info, axis=0)[:experts]
 
     hot = pick.reshape(2, ne // 4, 2, per, rows).transpose(1, 0, 2, 3, 4).reshape(ne // 4, 4 * per, rows)
     sv_send = jnp.dot(perm, saved_pre.reshape(total, 2 * half), preferred_element_type=F32).astype(BF)
     sv_send = sv_send.reshape(ne, per, 2 * half)
-    chosen_row = chosen.reshape(total, experts)
-    facts = jnp.concatenate([chosen_prob.reshape(-1, 1), is_low.reshape(-1, 1).astype(BF)], axis=1)
-    facts = jnp.pad(facts, ((0, 0), (0, 126)))
-    facts = jnp.dot(perm, facts, preferred_element_type=F32).astype(BF).reshape(ne, per, 128)
-    wide = ((0, 0), (0, 128 - experts))
-    hot_expert = jnp.dot(perm, jnp.pad(chosen_row.astype(BF), wide), preferred_element_type=F32).astype(BF)
-    base = (balance_coef * experts * counts.astype(F32) / total)[None, :]
+    facts = jnp.where(lane == experts, chosen_prob.reshape(-1, 1), info).astype(BF)
+    facts = jnp.dot(perm, facts, preferred_element_type=F32).astype(BF)
+    base = (balance_coef * experts * counts / total)[None, :]
     extra = 2.0 * zloss_coef * log_total[:, None] * router_probs
 
     _, part_back, sums, router_all, logits_grad = fused(
-        tokens, out_grad, sv_send, facts, hot, slot_weight[0], hot_expert, pick.T, jnp.pad(router_probs, wide),
+        tokens, out_grad, sv_send, facts.reshape(ne, per, 128), hot, slot_weight[0], facts, pick.T, wide_probs,
         jnp.pad(base, wide), jnp.pad(extra, wide), ne, nd)
     logits_grad = logits_grad[:, :experts]
     expert_part = lax.dot_general(pick, part_back.reshape(total, width), (((0,), (0,)), ((), ())),

time: 397 us -> 356 us (0.90)
  the two profiles are of different devices: /device:TPU:2 before, /device:TPU:100 now
where the time goes in v4:
time: 356 us; the launch traced here: 355 us
  Pallas kernels  327 us (92%)
  local copies, waits for them, and re-layouts  12.7 us (4%)
  matrix products  10.9 us (3%)
    pallas_call x1, Pallas kernels, fused(): pl.pallas_call(kernel, out_shape=[shape((2, nx, two, cols), BF), shape((n...  327 us

profile of v4, /device:TPU:100, one launch (start us, length us, event | category | flops | bytes accessed | tf_op | source)
XLA Modules:
  0.0 355.2 jit_solution(450303817935265375)
XLA Ops:
  0.6 0.0 copy-start
  0.6 0.0 copy-start.5
  0.7 1.0 copy-done
  1.7 1.7 fusion.29
  3.4 0.1 copy.36
  3.5 0.1 broadcast_multiply_fusion
  3.7 0.0 copy-start.3
  3.7 0.8 copy.35
  4.5 0.1 eq.94
  4.6 0.8 reshape.201
  5.4 0.1 slice_reduce_fusion
  5.5 0.1 broadcast_in_dim.51
  5.5 0.1 reshape.202
  5.6 0.7 eq.103
  6.3 1.2 fusion.28
  7.5 0.0 copy-start.7
  7.5 0.0 copy-done.5
  7.6 0.1 fusion.22
  7.8 0.1 copy.34
  7.9 0.1 eq.89
  8.0 1.6 fusion.11.he
  9.6 0.6 pad.12.ba
  10.2 0.6 pad.13.ex
  10.8 1.9 fusion.4
  12.8 0.7 copy.37
  13.5 0.0 copy-done.3
  13.5 0.8 copy.38
  14.4 0.0 copy-done.7
  14.4 3.7 %fusion.8 = bf16[1024,1024]{1,0:T(8,128)(2,1)} fusion(bf16[128,8,1024]{2,1,0:T(8,128)(2,1)S(1)} %copy-done.7, s32[1024]{0:T(1024)S(1)} %eq.89), kind=kOutput, calls=%fused_computation.11 | convolution fusion | flops 2149580800 | bytes 4198400 | tf_op jit(solution)/shard_map/dot_general | solution.py:662
  18.0 326.8 %shard_map.94 = (bf16[2,4,512,1536]{3,2,1,0:T(8,128)(2,1)}, bf16[32,32,2048]{2,1,0:T(8,128)(2,1)}, bf16[3,256,1024]{2,1,0:T(8,128)(2,1)}, f32[8,16,8,128]{3,2,1,0:T(8,128)}, f32[128,128]{1,0:T(8,128)}) custom-call(bf16[128,2048]{1,0:T(8,128)(2,1)} %tok.1, bf16[128,2048]{1,0:T(8,128)(2,1)} %og.1, bf16[32,32,1024]{2,1,0:T(8,128)(2,1)} %bitcast.43, ...), custom_call_target="tpu_custom_call" | custom-call | tf_op jit(solution)/shard_map/pallas_call | solution.py:597
  344.9 0.0 copy-start.6
  344.9 1.3 slice_bitcast_fusion.1
  346.2 1.1 slice_bitcast_fusion.3
  347.3 0.0 copy-done.6
  347.3 0.6 dynamic_slice.3
  348.5 0.3 broadcast_select_fusion.1
  348.8 0.0 copy-start.1
  348.8 0.1 pad_maximum_fusion
  349.0 2.8 copy.39
  351.7 0.0 copy-done.1
  351.7 0.0 copy-start.4
  351.7 0.7 fusion.30
  352.5 0.0 copy-start.2
  352.5 0.1 copy-done.4
  352.6 1.8 fusion.3
  354.4 0.0 copy-done.2
  354.4 0.8 copy.41
  (11 shorter events, 0.2 us)
Async XLA Ops:
  0.6 1.0 copy-start
  0.6 6.9 %copy-start.5 = (s32[128,8]{0,1:T(8,128)S(1)}, s32[128,8]{0,1:T(8,128)}, u32[]{:S(2)}) copy-start(s32[128,8]{0,1:T(8,128)} %param.12) | copy-start | bytes 12292
  3.7 9.8 %copy-start.3 = (f32[128,128]{1,0:T(8,128)}, f32[128,128]{1,0:T(8,128)S(1)}, u32[]{:S(2)}) copy-start(f32[128,128]{1,0:T(8,128)S(1)} %pad.11.pb) | copy-start | bytes 196612
  7.5 6.8 %copy-start.7 = (bf16[128,8,1024]{2,1,0:T(8,128)(2,1)S(1)}, bf16[128,8,1024]{2,1,0:T(8,128)(2,1)}, u32[]{:S(2)}) copy-start(bf16[128,8,1024]{2,1,0:T(8,128)(2,1)} %param.9) | copy-start | bytes 6291460
  344.9 2.4 copy-start.6
  348.8 2.9 copy-start.1
  351.7 0.8 copy-start.4
  352.5 1.9 copy-start.2
